TPU v7x, 256 devices: a whole 4x4x8 slice. The times are simulated.
256 devices in a mesh: xb: 16 (over z, y_lo), fsdp: 16 (over x, y_hi, core).
Axes of the slice: x: 4, y: 4 (y_hi: 2, y_lo: 2; y = y_hi * 2 + y_lo), z: 8, core: 2. Of those that a mesh axis runs over, the one named last changes fastest.
Arguments:
- tokens: bfloat16 [256, 128, 2048], P(('xb', 'fsdp')), may hold values from -24 to 24
- query_weight: bfloat16 [2048, 2048], P('fsdp'), may hold values from -0.125 to 0.125
- current_keys: bfloat16 [256, 128, 2048], P(('xb', 'fsdp')), may hold values from -6 to 6
- current_values: bfloat16 [256, 128, 2048], P(('xb', 'fsdp')), may hold values from -6 to 6
- cache_keys: bfloat16 [256, 512, 2048], P(('xb', 'fsdp')), may hold values from -480 to 480
- cache_values: bfloat16 [256, 512, 2048], P(('xb', 'fsdp')), may hold values from -6 to 6
- cache_fill: int32 [256], P(('xb', 'fsdp')), may hold values from 1 to 512, as said below
- document_group: int32 [256], replicated, may hold values from 0 to 1
- attended_grad: bfloat16 [256, 128, 2048], P(('xb', 'fsdp')), may hold values from -6 to 6
Outputs:
- attended: bfloat16 [256, 128, 2048], P(('xb', 'fsdp'))
- tokens_grad: bfloat16 [256, 128, 2048], P(('xb', 'fsdp'))
- keys_grad: bfloat16 [256, 128, 2048], P(('xb', 'fsdp'))
- values_grad: bfloat16 [256, 128, 2048], P(('xb', 'fsdp'))
- weight_grad: float32 [2048, 2048], P('fsdp')
Inputs may be any that keep to these rules, and one draw needn't show every extreme that they name: `cache_fill`: each document uses the first entries of its cache; some document uses all 512.
All inputs are finite; a program needn't handle non-finite values.
Results may differ from a plain program's by a relative error of at most 0.04.
Values may be sent and summed in bfloat16 or wider, within the bound.
No kernel may reach another device: no remote copies, remote signals or barrier semaphores. Data moves between devices by JAX's collectives and lax.ppermute only.
A program may use at most 128 MiB of HBM per device.

v0:
```python
import functools

import jax
import jax.numpy as jnp
from jax import lax
from jax.experimental import pallas as pl
from jax.experimental.pallas import tpu as pltpu
from jax.sharding import Mesh
from jax.sharding import PartitionSpec as P

HEADS = 16
HEAD = 128
SEQ = 128
NEG = -1e30
FLOOR = -1e29
SCALING = HEAD ** (-0.5)
LOG2E = 1.4426950408889634
XB = ("g", "q")
FS = ("x", "yh", "core")
BF = jnp.bfloat16
F32 = jnp.float32


def dot_nt(a, b):
    return lax.dot_general(a, b, (((1,), (1,)), ((), ())), preferred_element_type=F32)


def dot_nn(a, b):
    return lax.dot_general(a, b, (((1,), (0,)), ((), ())), preferred_element_type=F32)


def split3(x):
    hi = x.astype(BF)
    rest = x - hi.astype(F32)
    mid = rest.astype(BF)
    low = (rest - mid.astype(F32)).astype(BF)
    return hi, mid, low


def stat_rows(columns):
    lane = lax.broadcasted_iota(jnp.int32, (SEQ, SEQ), 1)
    tile = jnp.zeros((SEQ, SEQ), F32)
    for i, column in enumerate(columns):
        tile = jnp.where(lane == i, column, tile)
    return tile.T


def pack_rows(rows):
    hi, mid, low = split3(rows)
    blank = jnp.zeros((8, SEQ), F32)
    parts = [hi.astype(F32), mid.astype(F32), low.astype(F32), blank]
    return jnp.concatenate(parts, axis=0).astype(BF)


def unpack_rows(packed):
    x = packed.astype(F32)
    return x[0:8] + x[8:16] + x[16:24]


def cross_kernel(idx_ref, q_ref, kvg_ref, bias_ref, ab_ref, o_ref, k_s, v_s, kv_s, *, slots):
    docs = kvg_ref.shape[0]
    step = q_ref.shape[0]

    @pl.when(pl.program_id(0) == 0)
    def _():
        for m in range(docs):
            k = kvg_ref[m, 0]
            v = kvg_ref[m, 1]
            k_s[m * SEQ : (m + 1) * SEQ, :] = k
            v_s[m * SEQ : (m + 1) * SEQ, :] = v
            kv_s[m * SEQ : (m + 1) * SEQ, :HEAD] = v
            kv_s[m * SEQ : (m + 1) * SEQ, HEAD:] = k

    first = pl.program_id(0) * step
    slot = jnp.where(first < 4, slots[0], slots[1])
    docs_at = [
        4 * ((idx_ref[0] + 4 - slot) % 4) + (idx_ref[1] ^ ((first + j) % 4)) for j in range(step)
    ]
    q = q_ref[...].reshape(step * SEQ, HEAD)
    g = jnp.concatenate([kvg_ref[doc, 2] for doc in docs_at], axis=0)
    scores = dot_nt(q, k_s[...]) * (SCALING * LOG2E)
    scores = jnp.concatenate(
        [scores[j * SEQ : (j + 1) * SEQ] + bias_ref[docs_at[j]] for j in range(step)], axis=0
    )
    top = jnp.maximum(jnp.max(scores, axis=1, keepdims=True), FLOOR)
    weights = jnp.exp2(scores - top).astype(BF)
    weights32 = weights.astype(F32)
    total = jnp.sum(weights32, axis=1, keepdims=True)
    inverse = 1.0 / jnp.maximum(total, 0.5)
    both = dot_nn(weights, kv_s[...]) * inverse
    o = both[:, :HEAD]
    delta = jnp.sum(o * g.astype(F32), axis=1, keepdims=True)
    slope = (weights32 * (dot_nt(g, v_s[...]) - delta)).astype(BF)
    a = dot_nn(slope, k_s[...]) * inverse
    top = jnp.where(total > 0.0, top, NEG)
    for j in range(step):
        rows = slice(j * SEQ, (j + 1) * SEQ)
        packed = pack_rows(stat_rows([top[rows], total[rows], delta[rows]])[0:8, :])
        ab_ref[j, 0:SEQ, :] = a[rows].astype(BF)
        ab_ref[j, SEQ : 2 * SEQ, :] = both[rows, HEAD:].astype(BF)
        ab_ref[j, 2 * SEQ : 2 * SEQ + 32, :] = packed
        o_ref[j, 0:SEQ, :] = o[rows].astype(BF)
        o_ref[j, SEQ : SEQ + 32, :] = packed


def cross_attention(idx, q_heads, kvg, bias, slots):
    docs = kvg.shape[0]
    some = q_heads.shape[0]
    step = 2
    return pl.pallas_call(
        functools.partial(cross_kernel, slots=slots),
        grid_spec=pltpu.PrefetchScalarGridSpec(
            num_scalar_prefetch=1,
            grid=(some // step,),
            in_specs=[
                pl.BlockSpec((step, SEQ, HEAD), lambda i, x: (i, 0, 0)),
                pl.BlockSpec((docs, 3, SEQ, HEAD), lambda i, x: (0, 0, 0, 0)),
                pl.BlockSpec((docs, 1, docs * SEQ), lambda i, x: (0, 0, 0)),
            ],
            out_specs=[
                pl.BlockSpec((step, 2 * SEQ + 32, HEAD), lambda i, x: (i, 0, 0)),
                pl.BlockSpec((step, SEQ + 32, HEAD), lambda i, x: (i, 0, 0)),
            ],
            scratch_shapes=[
                pltpu.VMEM((docs * SEQ, HEAD), BF),
                pltpu.VMEM((docs * SEQ, HEAD), BF),
                pltpu.VMEM((docs * SEQ, 2 * HEAD), BF),
            ],
        ),
        out_shape=[
            jax.ShapeDtypeStruct((some, 2 * SEQ + 32, HEAD), BF),
            jax.ShapeDtypeStruct((some, SEQ + 32, HEAD), BF),
        ],
        compiler_params=pltpu.CompilerParams(vmem_limit_bytes=40 * 2**20),
        cost_estimate=pl.CostEstimate(
            flops=some * SEQ * SEQ, bytes_accessed=2**16, transcendentals=0
        ),
        name="cross",
    )(idx, q_heads, kvg, bias)


def by_heads_kernel(*refs):
    out_ref = refs[3]
    for c in range(4):
        for i in range(3):
            out_ref[c, i] = refs[i][0, :, c * HEAD : (c + 1) * HEAD]


def by_heads(*arrays):
    block = pl.BlockSpec((1, SEQ, 4 * HEAD), lambda i: (0, 0, i))
    return pl.pallas_call(
        by_heads_kernel,
        grid=(4,),
        in_specs=[block] * 3,
        out_specs=pl.BlockSpec((4, 3, SEQ, HEAD), lambda i: (i, 0, 0, 0)),
        out_shape=jax.ShapeDtypeStruct((HEADS, 3, SEQ, HEAD), BF),
        cost_estimate=pl.CostEstimate(flops=0, bytes_accessed=3 * 2**20, transcendentals=0),
        name="by_heads",
    )(*arrays)


def own_kernel(
    idx_ref, q_ref, g_ref, ck_ref, cv_ref, lk_ref, lv_ref, ab_ref, o_ref, s_ref
):
    cache = ck_ref.shape[1]
    entry = lax.broadcasted_iota(jnp.int32, (SEQ, cache), 1)
    row = lax.broadcasted_iota(jnp.int32, (SEQ, SEQ), 0)
    col = lax.broadcasted_iota(jnp.int32, (SEQ, SEQ), 1)
    for c in range(4):
        cols = slice(c * HEAD, (c + 1) * HEAD)
        k = idx_ref[1] ^ c
        q = q_ref[k]
        g = g_ref[0, :, cols]
        ck, cv = ck_ref[0, :, cols], cv_ref[0, :, cols]
        lk, lv = lk_ref[0, :, cols], lv_ref[0, :, cols]
        stale = jnp.where(entry < idx_ref[2], dot_nt(q, ck) * (SCALING * LOG2E), NEG)
        local = jnp.where(col <= row, dot_nt(q, lk) * (SCALING * LOG2E), NEG)
        top = jnp.maximum(
            jnp.max(stale, axis=1, keepdims=True), jnp.max(local, axis=1, keepdims=True)
        )
        ws = jnp.exp2(stale - top).astype(BF)
        wl = jnp.exp2(local - top).astype(BF)
        ws32 = ws.astype(F32)
        wl32 = wl.astype(F32)
        total = jnp.sum(ws32, axis=1, keepdims=True) + jnp.sum(wl32, axis=1, keepdims=True)
        inverse = 1.0 / total
        o = (dot_nn(ws, cv) + dot_nn(wl, lv)) * inverse
        b = (dot_nn(ws, ck) + dot_nn(wl, lk)) * inverse
        delta = jnp.sum(o * g.astype(F32), axis=1, keepdims=True)
        ss = (ws32 * (dot_nt(g, cv) - delta)).astype(BF)
        sl = (wl32 * (dot_nt(g, lv) - delta)).astype(BF)
        a = (dot_nn(ss, ck) + dot_nn(sl, lk)) * inverse
        rows = stat_rows([top, total, delta])[0:8, :]
        ab_ref[k, 0:SEQ, :] = a.astype(BF)
        ab_ref[k, SEQ : 2 * SEQ, :] = b.astype(BF)
        ab_ref[k, 2 * SEQ : 2 * SEQ + 32, :] = pack_rows(rows)
        o_ref[:, cols] = o
        s_ref[c] = rows


def own_attention(idx, q_own, grad, cache_k, cache_v, local_k, local_v):
    cache = cache_k.shape[1]
    width = HEADS * HEAD
    head_block = pl.BlockSpec((1, SEQ, 4 * HEAD), lambda j, x: (0, 0, (x[0] + j) % 4))
    cache_block = pl.BlockSpec((1, cache, 4 * HEAD), lambda j, x: (0, 0, (x[0] + j) % 4))
    return pl.pallas_call(
        own_kernel,
        grid_spec=pltpu.PrefetchScalarGridSpec(
            num_scalar_prefetch=1,
            grid=(4,),
            in_specs=[
                pl.BlockSpec((4, SEQ, HEAD), lambda j, x: (0, 0, j)),
                head_block,
                cache_block,
                cache_block,
                head_block,
                head_block,
            ],
            out_specs=[
                pl.BlockSpec((4, 2 * SEQ + 32, HEAD), lambda j, x: (0, 0, j)),
                pl.BlockSpec((SEQ, 4 * HEAD), lambda j, x: (0, (x[0] + j) % 4)),
                pl.BlockSpec((4, 8, SEQ), lambda j, x: ((x[0] + j) % 4, 0, 0)),
            ],
        ),
        out_shape=[
            jax.ShapeDtypeStruct((4, 2 * SEQ + 32, 4 * HEAD), BF),
            jax.ShapeDtypeStruct((SEQ, width), F32),
            jax.ShapeDtypeStruct((HEADS, 8, SEQ), F32),
        ],
        compiler_params=pltpu.CompilerParams(vmem_limit_bytes=24 * 2**20),
        cost_estimate=pl.CostEstimate(
            flops=cache * SEQ, bytes_accessed=2**16, transcendentals=0
        ),
        name="own",
    )(idx, q_own, grad, cache_k, cache_v, local_k, local_v)


def merge_rows(x_top, x_total, x_delta, o_top, o_total, o_delta):
    big = jnp.maximum(x_top, o_top)
    x_share = jnp.exp2(x_top - big)
    o_share = jnp.exp2(o_top - big)
    inverse = 1.0 / (x_share * x_total + o_share * o_total)
    x_weight = x_share * x_total * inverse
    o_weight = o_share * o_total * inverse
    delta = x_weight * x_delta + o_weight * o_delta
    return x_weight, o_weight, delta, o_share * inverse


def dest_kernel(*refs):
    x_refs, y_refs, qg_ref = refs[0:4], refs[4:8], refs[8]
    base = 2 * SEQ
    xs = [unpack_rows(x_refs[j][k, base : base + 32, :]) for k in range(4) for j in range(4)]
    ys = [
        unpack_rows(y_refs[k][base : base + 32, j * HEAD : (j + 1) * HEAD])
        for k in range(4)
        for j in range(4)
    ]
    x_stat = [jnp.concatenate([t[i : i + 1] for t in xs], axis=0) for i in range(3)]
    y_stat = [jnp.concatenate([t[i : i + 1] for t in ys], axis=0) for i in range(3)]
    x_weight, o_weight, delta, _ = merge_rows(*x_stat, *y_stat)
    rows = [
        x_weight * SCALING,
        x_weight * (x_stat[2] - delta) * SCALING,
        o_weight * SCALING,
        o_weight * (y_stat[2] - delta) * SCALING,
    ]
    tile = jnp.concatenate([*rows, jnp.zeros((SEQ - 64, SEQ), F32)], axis=0).T
    for k in range(4):
        for j in range(4):
            c = k * 4 + j
            cols = slice(j * HEAD, (j + 1) * HEAD)
            grad = (
                tile[:, c : c + 1] * x_refs[j][k, 0:SEQ, :].astype(F32)
                + tile[:, 16 + c : 17 + c] * x_refs[j][k, SEQ:base, :].astype(F32)
                + tile[:, 32 + c : 33 + c] * y_refs[k][0:SEQ, cols].astype(F32)
                + tile[:, 48 + c : 49 + c] * y_refs[k][SEQ:base, cols].astype(F32)
            )
            qg_ref[k * SEQ : (k + 1) * SEQ, cols] = grad.astype(BF)


def dest_combine(xs, ys):
    return pl.pallas_call(
        dest_kernel,
        out_shape=jax.ShapeDtypeStruct((4 * SEQ, 4 * HEAD), BF),
        compiler_params=pltpu.CompilerParams(vmem_limit_bytes=24 * 2**20),
        cost_estimate=pl.CostEstimate(
            flops=8 * 16 * SEQ * HEAD, bytes_accessed=3 * 2**20, transcendentals=0
        ),
        name="dest",
    )(*xs, *ys)


def finish_kernel(
    idx_ref, x_ref, o_ref, s_ref, q_ref, g_ref, lk_ref, lv_ref, att_ref, kg_ref, vg_ref
):
    key = lax.broadcasted_iota(jnp.int32, (SEQ, SEQ), 0)
    query = lax.broadcasted_iota(jnp.int32, (SEQ, SEQ), 1)
    for c in range(4):
        cols = slice(c * HEAD, (c + 1) * HEAD)
        k = idx_ref[1] ^ c
        q = q_ref[k]
        g = g_ref[0, :, cols]
        xr = unpack_rows(x_ref[k, 0, SEQ : SEQ + 32, :])
        yr = s_ref[c]
        x_weight, o_weight, delta, factor = merge_rows(
            xr[0:1], xr[1:2], xr[2:3], yr[0:1], yr[1:2], yr[2:3]
        )
        pair = jnp.concatenate([x_weight, o_weight, jnp.zeros((SEQ - 2, SEQ), F32)], axis=0).T
        att_ref[0, :, cols] = (
            pair[:, 0:1] * x_ref[k, 0, 0:SEQ, :].astype(F32) + pair[:, 1:2] * o_ref[:, cols]
        ).astype(BF)
        scores = dot_nt(lk_ref[0, :, cols], q) * (SCALING * LOG2E)
        scores = jnp.where(key <= query, scores, NEG)
        prob = jnp.exp2(scores - yr[0:1]).astype(BF).astype(F32) * factor
        slope = (prob * (dot_nt(lv_ref[0, :, cols], g) - delta)).astype(BF)
        vg_ref[0, :, cols] = dot_nn(prob.astype(BF), g).astype(BF)
        kg_ref[0, :, cols] = (dot_nn(slope, q) * SCALING).astype(BF)


def finish(idx, returned, o, stats, q_own, grad, local_k, local_v):
    width = HEADS * HEAD
    row_block = pl.BlockSpec((1, SEQ, 4 * HEAD), lambda i, x: (0, 0, i))
    return pl.pallas_call(
        finish_kernel,
        grid_spec=pltpu.PrefetchScalarGridSpec(
            num_scalar_prefetch=1,
            grid=(4,),
            in_specs=[
                pl.BlockSpec((4, 1, SEQ + 32, HEAD), lambda i, x: (0, (i + 4 - x[0]) % 4, 0, 0)),
                pl.BlockSpec((SEQ, 4 * HEAD), lambda i, x: (0, i)),
                pl.BlockSpec((4, 8, SEQ), lambda i, x: (i, 0, 0)),
                pl.BlockSpec((4, SEQ, HEAD), lambda i, x: (0, 0, (i + 4 - x[0]) % 4)),
                row_block,
                row_block,
                row_block,
            ],
            out_specs=[row_block, row_block, row_block],
        ),
        out_shape=[jax.ShapeDtypeStruct((1, SEQ, width), BF)] * 3,
        compiler_params=pltpu.CompilerParams(vmem_limit_bytes=24 * 2**20),
        cost_estimate=pl.CostEstimate(
            flops=10 * SEQ * SEQ * width,
            bytes_accessed=5 * 2**20,
            transcendentals=SEQ * SEQ * HEADS,
        ),
        name="finish",
    )(idx, returned, o, stats, q_own, grad, local_k, local_v)


def place_kernel(idx_ref, *refs):
    out_ref = refs[4]
    for k in range(4):
        for j in range(4):
            head = 4 * ((idx_ref[0] + j) % 4) + (idx_ref[1] ^ k)
            start = pl.multiple_of(head * HEAD, HEAD)
            out_ref[:, pl.ds(start, HEAD)] = refs[k][:, j * HEAD : (j + 1) * HEAD].astype(F32)


def place(idx, parts):
    rows = parts[0].shape[0]
    return pl.pallas_call(
        place_kernel,
        in_specs=[pl.BlockSpec(memory_space=pltpu.SMEM)] + [pl.BlockSpec()] * 4,
        out_shape=jax.ShapeDtypeStruct((rows, HEADS * HEAD), F32),
        cost_estimate=pl.CostEstimate(flops=0, bytes_accessed=2 * 2**20, transcendentals=0),
        name="place",
    )(idx, *parts)


def a2a(x, axis):
    return lax.all_to_all(x, axis, 0, 0, tiled=True)


def shift(x, axis, k):
    return lax.ppermute(x, axis, [(s, (s + k) % 4) for s in range(4)]) if k % 4 else x


def swap(x, axis, k):
    return lax.ppermute(x, axis, [(s, s ^ k) for s in range(4)]) if k else x


def in_order(mine, other, first, axis):
    return jnp.stack([jnp.where(first, mine, other), jnp.where(first, other, mine)], axis=axis)


def gather_shards(shard, tok1, tok2):
    x_index = lax.axis_index("x")
    slots = jnp.stack([shift(shard, "x", -k) for k in range(4)])
    slots = jnp.where(x_index % 2 == 1, jnp.roll(slots, 1, axis=0), slots)
    slots = jnp.where(x_index >= 2, jnp.roll(slots, 2, axis=0), slots)
    slots, tok1, tok2 = lax.optimization_barrier((slots, tok1, tok2))
    tok3 = swap(tok2, "q", 1)
    other = lax.ppermute(slots, "yh", [(0, 1), (1, 0)])
    slots = in_order(slots, other, lax.axis_index("yh") == 0, 1)
    slots, tok3 = lax.optimization_barrier((slots, tok3))
    other = lax.ppermute(slots, "core", [(0, 1), (1, 0)])
    slots = in_order(slots, other, lax.axis_index("core") == 0, 2)
    return slots.reshape(16 * shard.shape[0], -1), tok1, tok2, tok3


def body(
    tokens,
    query_weight,
    current_keys,
    current_values,
    cache_keys,
    cache_values,
    cache_fill,
    document_group,
    attended_grad,
):
    g_index = lax.axis_index("g")
    q_index = lax.axis_index("q")
    col_index = lax.axis_index(FS)
    idx = jnp.stack([g_index, q_index, cache_fill[0]]).astype(jnp.int32)

    own_tok = tokens[0]
    tok2, tok1 = swap(own_tok, "q", 2), swap(own_tok, "q", 1)
    kvg = by_heads(current_keys, current_values, attended_grad)
    quarter = jnp.concatenate(
        [
            lax.dynamic_slice_in_dim(
                query_weight, (4 * ((g_index + j) % 4) + q_index) * HEAD, HEAD, axis=1
            )
            for j in range(4)
        ],
        axis=1,
    )
    weight, tok1, tok2, tok3 = gather_shards(quarter, tok1, tok2)

    kvg = a2a(kvg, XB)

    tok = jnp.concatenate([own_tok, tok1, tok2, tok3])
    queries = jnp.dot(tok, weight, preferred_element_type=F32).astype(BF)
    later, kvg = lax.optimization_barrier((queries, kvg))
    by_slot = [queries[:, j * HEAD : (j + 1) * HEAD] for j in range(4)]
    q_heads = [shift(by_slot[j], "g", j).reshape(4, SEQ, HEAD) for j in range(4)]
    q_own = jnp.stack([swap(later[k * SEQ : (k + 1) * SEQ], "q", k) for k in range(4)])

    labels = lax.dynamic_index_in_dim(
        document_group.reshape(16, 16), col_index, axis=1, keepdims=False
    )
    number = jnp.arange(16)
    valid = (labels[:, None] == labels[None, :]) & (number[:, None] != number[None, :])
    bias = jnp.repeat(jnp.where(valid, 0.0, NEG).astype(F32), SEQ, axis=1)[:, None, :]

    ab, out = [None] * 4, [None] * 4
    halves = ((2, 0), (1, 3))
    two = [jnp.concatenate([q_heads[j] for j in slots]) for slots in halves]

    def cross_half(n):
        both, outs = cross_attention(idx, two[n], kvg, bias, halves[n])
        for i, j in enumerate(halves[n]):
            ab[j], out[j] = both[4 * i : 4 * i + 4], outs[4 * i : 4 * i + 4]
        return both

    q_own, _ = lax.optimization_barrier((q_own, cross_half(0)))
    up, down = shift(ab[2][:2], "g", -1), shift(ab[2][2:], "g", 1)
    own_ab, o, stats = own_attention(
        idx, q_own, attended_grad, cache_keys, cache_values, current_keys, current_values
    )
    two[1], stats, up, down = lax.optimization_barrier((two[1], stats, up, down))
    up, down = shift(up, "g", -1), shift(down, "g", 1)
    xs = [ab[0], None, jnp.concatenate([up, down]), None]
    ys = [swap(own_ab[k], "q", k) for k in range(4)]
    cross_half(1)
    xs[1], xs[3] = shift(ab[1], "g", -1), shift(ab[3], "g", -3)
    qg = dest_combine(xs, ys)

    partial = lax.dot_general(
        tok, qg, (((0,), (0,)), ((), ())), preferred_element_type=F32
    ).astype(BF)
    pieces = a2a(partial.reshape(16, query_weight.shape[0], 4 * HEAD), FS)
    mine = jnp.sum(pieces.astype(F32), axis=0).astype(BF)

    part = dot_nt(qg, weight).astype(BF).reshape(2, 2, SEQ, -1)
    swapped, _ = lax.optimization_barrier((swap(part[:, 1], "q", 1), mine))
    near = part[:, 0].astype(F32) + swapped.astype(F32)
    tokens_grad = near[0] + swap(near[1].astype(BF), "q", 2).astype(F32)
    tokens_grad = tokens_grad.astype(BF)[None]

    out, _ = lax.optimization_barrier((out, partial))
    over_g = [shift(out[j], "g", -j) for j in range(4)]
    over_g, _ = lax.optimization_barrier((over_g, mine))
    returned = jnp.stack(
        [swap(jnp.stack([over_g[j][k] for j in range(4)]), "q", k) for k in range(4)]
    )
    attended, keys_grad, values_grad = finish(
        idx, returned, o, stats, q_own, attended_grad, current_keys, current_values
    )

    summed = sum(
        jnp.roll(shift(mine, "g", k), -k * HEAD, axis=1).astype(F32) for k in range(4)
    ).astype(BF)
    weight_grad = place(idx, [swap(summed, "q", k) for k in range(4)])
    return attended, tokens_grad, keys_grad, values_grad, weight_grad


def solution(mesh):
    grid = Mesh(mesh.devices.reshape(4, 4, 4, 2, 2), XB + FS)
    docs = P(XB + FS, None, None)
    in_specs = (docs, P(FS, None), docs, docs, docs, docs, P(XB + FS), P(), docs)
    out_specs = (docs, docs, docs, docs, P(FS, None))
    return jax.shard_map(body, mesh=grid, in_specs=in_specs, out_specs=out_specs, check_vma=False)
```

profile of v0, /device:TPU:48, one launch (start us, length us, event | category | flops | bytes accessed | tf_op | source)
XLA Modules:
  0.0 248.4 jit_solution(442292867755411514)
XLA Ops:
  1.6 2.8 %collective-permute-start.1 = (bf16[128,512]{1,0:T(8,128)(2,1)S(1)}, bf16[128,512]{1,0:T(8,128)(2,1)S(1)}, u32[]{:S(2)}, u32[]{:S(2)}) collective-permute-start(bf16[128,512]{1,0:T(8,128)(2,1)S(1)} %get-tuple-element.116), channel_id=1, source_target_pairs={{0,12},{4,0},{8,4},{12,8},{1,13},{5,1},{9,5},{13,9},{2,14},{6,2},{... | collective-permute-start | bytes 393224 | tf_op jit(solution)/shard_map/ppermute | solution.py:375
  7.5 2.5 %collective-permute-done.1 = bf16[128,512]{1,0:T(8,128)(2,1)S(1)} collective-permute-done((bf16[128,512]{1,0:T(8,128)(2,1)S(1)}, bf16[128,512]{1,0:T(8,128)(2,1)S(1)}, u32[]{:S(2)}, u32[]{:S(2)}) %collective-permute-start.1) | collective-permute-done | bytes 131104 | tf_op jit(solution)/shard_map/ppermute | solution.py:375
  14.0 5.2 %collective-permute-done.4 = bf16[128,2048]{1,0:T(8,128)(2,1)} collective-permute-done((bf16[128,2048]{1,0:T(8,128)(2,1)}, bf16[128,2048]{1,0:T(8,128)(2,1)}, u32[]{:S(2)}, u32[]{:S(2)}) %collective-permute-start.4) | collective-permute-done | bytes 524320 | tf_op jit(solution)/shard_map/ppermute | solution.py:379
  21.7 3.7 %by_heads.1 = bf16[16,3,128,128]{3,2,1,0:T(8,128)(2,1)} custom-call(bf16[1,128,2048]{2,1,0:T(8,128)(2,1)} %lk_ref.3, bf16[1,128,2048]{2,1,0:T(8,128)(2,1)} %lv_ref.3, bf16[1,128,2048]{2,1,0:T(8,128)(2,1)} %g_ref.3), custom_call_target="tpu_custom_call" | custom-call | bytes 3145728 | tf_op jit(solution)/shard_map/by_heads/pallas_call | solution.py:151
  25.5 9.2 %all-to-all-start = ((bf16[16,3,128,128]{3,2,1,0:T(8,128)(2,1)}), bf16[16,3,128,128]{3,2,1,0:T(8,128)(2,1)S(1)}, u32[]{:S(2)}, u32[]{:S(2)}) async-start(bf16[16,3,128,128]{3,2,1,0:T(8,128)(2,1)} %by_heads.1), calls=%async_computation | async-start | bytes 3145728 | tf_op jit(solution)/shard_map/all_to_all | solution.py:371
  35.8 9.3 %collective-permute-done.6 = bf16[128,2048]{1,0:T(8,128)(2,1)} collective-permute-done((bf16[128,2048]{1,0:T(8,128)(2,1)}, bf16[128,2048]{1,0:T(8,128)(2,1)}, u32[]{:S(2)}, u32[]{:S(2)}) %collective-permute-start.6) | collective-permute-done | bytes 524320 | tf_op jit(solution)/shard_map/ppermute | solution.py:379
  45.3 2.5 %collective-permute-done.7 = bf16[4,2,128,512]{3,2,1,0:T(8,128)(2,1)} collective-permute-done((bf16[4,2,128,512]{3,2,1,0:T(8,128)(2,1)S(1)}, bf16[4,2,128,512]{3,2,1,0:T(8,128)(2,1)}, u32[]{:S(2)}, u32[]{:S(2)}) %collective-permute-start.7) | collective-permute-done | bytes 1048608 | tf_op jit(solution)/shard_map/ppermute | solution.py:396
  50.6 2.5 convolution_convert_fusion.2
  55.5 5.2 %collective-permute-start.10 = (bf16[512,128]{1,0:T(8,128)(2,1)S(1)}, bf16[512,128]{1,0:T(8,128)(2,1)S(1)}, u32[]{:S(2)}, u32[]{:S(2)}) collective-permute-start(bf16[512,128]{1,0:T(8,128)(2,1)S(1)} %get-tuple-element.84), channel_id=1, source_target_pairs={{0,192},{64,0},{128,64},{192,128},{1,193},{65,1},{129,65},{193,129... | collective-permute-start | bytes 393224 | tf_op jit(solution)/shard_map/ppermute | solution.py:375
  61.4 3.1 %collective-permute-start.8 = (bf16[512,128]{1,0:T(8,128)(2,1)S(1)}, bf16[512,128]{1,0:T(8,128)(2,1)S(1)}, u32[]{:S(2)}, u32[]{:S(2)}) collective-permute-start(bf16[512,128]{1,0:T(8,128)(2,1)S(1)} %get-tuple-element.86), channel_id=1, source_target_pairs={{0,128},{64,192},{128,0},{192,64},{1,129},{65,193},{129,1},{193,65... | collective-permute-start | bytes 393224 | tf_op jit(solution)/shard_map/ppermute | solution.py:375
  64.5 9.6 %collective-permute-done.9 = bf16[512,128]{1,0:T(8,128)(2,1)S(1)} collective-permute-done((bf16[512,128]{1,0:T(8,128)(2,1)S(1)}, bf16[512,128]{1,0:T(8,128)(2,1)S(1)}, u32[]{:S(2)}, u32[]{:S(2)}) %collective-permute-start.9) | collective-permute-done | bytes 131104 | tf_op jit(solution)/shard_map/ppermute | solution.py:375
  75.1 6.9 %collective-permute-done.8 = bf16[512,128]{1,0:T(8,128)(2,1)S(1)} collective-permute-done((bf16[512,128]{1,0:T(8,128)(2,1)S(1)}, bf16[512,128]{1,0:T(8,128)(2,1)S(1)}, u32[]{:S(2)}, u32[]{:S(2)}) %collective-permute-start.8) | collective-permute-done | bytes 131104 | tf_op jit(solution)/shard_map/ppermute | solution.py:375
  86.0 8.6 %cross.2 = (bf16[8,288,128]{2,1,0:T(8,128)(2,1)S(1)}, bf16[8,160,128]{2,1,0:T(8,128)(2,1)S(1)}) custom-call(s32[3]{0:T(128)S(1)} %pad_add_fusion.idx_ref, bf16[8,128,128]{2,1,0:T(8,128)(2,1)S(1)} %pad_maximum_fusion.8.q_ref, bf16[16,3,128,128]{3,2,1,0:T(8,128)(2,1)S(1)} %all-to-all-done.kvg_ref, f32[16,1,2048]{2,1,0:T(1,128)S(1)} %bitcast.73), custom_call_target="tpu_custom_call" | custom-call | flops 131072 | bytes 65536 | tf_op jit(solution)/shard_map/cross/pallas_call | solution.py:110
  94.8 4.1 %collective-permute-start.14 = (bf16[2,288,128]{2,1,0:T(8,128)(2,1)S(1)}, bf16[2,288,128]{2,1,0:T(8,128)(2,1)S(1)}, u32[]{:S(2)}, u32[]{:S(2)}) collective-permute-start(bf16[2,288,128]{2,1,0:T(8,128)(2,1)S(1)} %get-tuple-element.78), channel_id=1, source_target_pairs={{0,192},{64,0},{128,64},{192,128},{1,193},{65,1},{129,65},{193,129... | collective-permute-start | bytes 442376 | tf_op jit(solution)/shard_map/ppermute | solution.py:375
  100.6 11.3 %own.1 = (bf16[4,288,512]{2,1,0:T(8,128)(2,1)S(1)}, f32[128,2048]{1,0:T(8,128)S(1)}, f32[16,8,128]{2,1,0:T(8,128)S(1)}) custom-call(s32[3]{0:T(128)S(1)} %pad_add_fusion.idx_ref, bf16[4,128,512]{2,1,0:T(8,128)(2,1)S(1)} %pad_maximum_fusion.4.q_ref, bf16[1,128,2048]{2,1,0:T(8,128)(2,1)S(1)} %copy-done.2, bf16[1,512,2048]{2,1,0:T(8,128)(2,1)S(1)} %copy-done.4, ...), custom_call_target="tpu_custom_call" | custom-call | flops 65536 | bytes 65536 | tf_op jit(solution)/shard_map/own/pallas_call | solution.py:206
  116.4 8.6 %cross.3 = (bf16[8,288,128]{2,1,0:T(8,128)(2,1)S(1)}, bf16[8,160,128]{2,1,0:T(8,128)(2,1)S(1)}) custom-call(s32[3]{0:T(128)S(1)} %pad_add_fusion.idx_ref, bf16[8,128,128]{2,1,0:T(8,128)(2,1)S(1)} %pad_maximum_fusion.9.q_ref, bf16[16,3,128,128]{3,2,1,0:T(8,128)(2,1)S(1)} %all-to-all-done.kvg_ref, f32[16,1,2048]{2,1,0:T(1,128)S(1)} %bitcast.74), custom_call_target="tpu_custom_call" | custom-call | flops 131072 | bytes 65536 | tf_op jit(solution)/shard_map/cross/pallas_call | solution.py:110
  125.0 2.9 %collective-permute-start.18 = (bf16[2,288,128]{2,1,0:T(8,128)(2,1)S(1)}, bf16[2,288,128]{2,1,0:T(8,128)(2,1)S(1)}, u32[]{:S(2)}, u32[]{:S(2)}) collective-permute-start(bf16[2,288,128]{2,1,0:T(8,128)(2,1)S(1)} %collective-permute-done.15), channel_id=1, source_target_pairs={{0,64},{64,128},{128,192},{192,0},{1,65},{65,129},{129,193},{193,1... | collective-permute-start | bytes 442376 | tf_op jit(solution)/shard_map/ppermute | solution.py:375
  128.0 4.6 %collective-permute-done.17 = bf16[2,288,128]{2,1,0:T(8,128)(2,1)S(1)} collective-permute-done((bf16[2,288,128]{2,1,0:T(8,128)(2,1)S(1)}, bf16[2,288,128]{2,1,0:T(8,128)(2,1)S(1)}, u32[]{:S(2)}, u32[]{:S(2)}) %collective-permute-start.17) | collective-permute-done | bytes 147488 | tf_op jit(solution)/shard_map/ppermute | solution.py:375
  132.6 5.6 %collective-permute-done.18 = bf16[2,288,128]{2,1,0:T(8,128)(2,1)S(1)} collective-permute-done((bf16[2,288,128]{2,1,0:T(8,128)(2,1)S(1)}, bf16[2,288,128]{2,1,0:T(8,128)(2,1)S(1)}, u32[]{:S(2)}, u32[]{:S(2)}) %collective-permute-start.18) | collective-permute-done | bytes 147488 | tf_op jit(solution)/shard_map/ppermute | solution.py:375
  138.2 10.7 %collective-permute-start.16 = (bf16[4,288,128]{2,1,0:T(8,128)(2,1)S(1)}, bf16[4,288,128]{2,1,0:T(8,128)(2,1)S(1)}, u32[]{:S(2)}, u32[]{:S(2)}) collective-permute-start(bf16[4,288,128]{2,1,0:T(8,128)(2,1)S(1)} %get-tuple-element.76), channel_id=1, source_target_pairs={{0,192},{64,0},{128,64},{192,128},{1,193},{65,1},{129,65},{193,129... | collective-permute-start | bytes 884744 | tf_op jit(solution)/shard_map/ppermute | solution.py:375
  149.1 6.9 %collective-permute-done.16.refs_1_ = bf16[4,288,128]{2,1,0:T(8,128)(2,1)S(1)} collective-permute-done((bf16[4,288,128]{2,1,0:T(8,128)(2,1)S(1)}, bf16[4,288,128]{2,1,0:T(8,128)(2,1)S(1)}, u32[]{:S(2)}, u32[]{:S(2)}) %collective-permute-start.16) | collective-permute-done | bytes 294944 | tf_op jit(solution)/shard_map/ppermute | solution.py:375
  157.4 3.9 %convolution_convert_fusion.1 = bf16[2048,512]{1,0:T(8,128)(2,1)} fusion(bf16[512,512]{1,0:T(8,128)(2,1)S(1)} %dest.1, bf16[128,2048]{1,0:T(8,128)(2,1)} %collective-permute-done.6, bf16[128,2048]{1,0:T(8,128)(2,1)} %collective-permute-done.4, bf16[128,2048]{1,0:T(8,128)(2,1)S(1)} %copy-done.25, bf16[128,2048]{1,0:T(8,128)(2,1)S(1)} %bitcast.99), kind=kOutput, calls=%fused_computation.1 | convolution fusion | flops 1083179008 | bytes 4718592 | tf_op jit(solution)/shard_map/dot_general | solution.py:470
  161.2 6.7 %all-to-all-start.1 = ((bf16[16,128,512]{2,1,0:T(8,128)(2,1)}), bf16[16,128,512]{2,1,0:T(8,128)(2,1)}, u32[]{:S(2)}, u32[]{:S(2)}) async-start(bf16[16,128,512]{2,1,0:T(8,128)(2,1)} %bitcast.77), calls=%async_computation.1 | async-start | bytes 4194304 | tf_op jit(solution)/shard_map/all_to_all | solution.py:371
  168.7 2.9 %convolution_convert_fusion = bf16[512,2048]{1,0:T(8,128)(2,1)S(1)} fusion(bf16[512,512]{1,0:T(8,128)(2,1)S(1)} %dest.1, bf16[2048,512]{1,0:T(8,128)(2,1)} %bitcast.76), kind=kOutput, calls=%fused_computation | convolution fusion | flops 1074790400 | bytes 4718592 | tf_op jit(solution)/shard_map/dot_general | solution.py:25
  176.4 4.5 %collective-permute-start.24 = (bf16[4,160,128]{2,1,0:T(8,128)(2,1)}, bf16[4,160,128]{2,1,0:T(8,128)(2,1)S(1)}, u32[]{:S(2)}, u32[]{:S(2)}) collective-permute-start(bf16[4,160,128]{2,1,0:T(8,128)(2,1)} %get-tuple-element.55), channel_id=1, source_target_pairs={{0,128},{64,192},{128,0},{192,64},{1,129},{65,193},{129,1},{193,65... | collective-permute-start | bytes 491528 | tf_op jit(solution)/shard_map/ppermute | solution.py:375
  180.9 15.8 %all-to-all-done.1 = bf16[16,128,512]{2,1,0:T(8,128)(2,1)} async-done(((bf16[16,128,512]{2,1,0:T(8,128)(2,1)}), bf16[16,128,512]{2,1,0:T(8,128)(2,1)}, u32[]{:S(2)}, u32[]{:S(2)}) %all-to-all-start.1) | async-done | bytes 2097184 | tf_op jit(solution)/shard_map/all_to_all | solution.py:371
  198.7 2.4 collective-permute-start.33
  201.1 3.8 %collective-permute-start.32 = (bf16[128,512]{1,0:T(8,128)(2,1)S(1)}, bf16[128,512]{1,0:T(8,128)(2,1)S(1)}, u32[]{:S(2)}, u32[]{:S(2)}) collective-permute-start(bf16[128,512]{1,0:T(8,128)(2,1)S(1)} %reduce_sum.12), channel_id=1, source_target_pairs={{0,128},{64,192},{128,0},{192,64},{1,129},{65,193},{129,1},{193,65... | collective-permute-start | bytes 393224 | tf_op jit(solution)/shard_map/ppermute | solution.py:375
  207.4 9.4 %collective-permute-done.29 = bf16[2,128,2048]{2,1,0:T(8,128)(2,1)} collective-permute-done((bf16[2,128,2048]{2,1,0:T(8,128)(2,1)S(1)}, bf16[2,128,2048]{2,1,0:T(8,128)(2,1)}, u32[]{:S(2)}, u32[]{:S(2)}) %collective-permute-start.29) | collective-permute-done | bytes 1048608 | tf_op jit(solution)/shard_map/ppermute | solution.py:379
  221.3 3.0 %collective-permute-start.36 = (bf16[128,512]{1,0:T(8,128)(2,1)S(1)}, bf16[128,512]{1,0:T(8,128)(2,1)S(1)}, u32[]{:S(2)}, u32[]{:S(2)}) collective-permute-start(bf16[128,512]{1,0:T(8,128)(2,1)S(1)} %add_convert_fusion.refs_0_), channel_id=1, source_target_pairs={{0,48},{16,32},{32,16},{48,0},{1,49},{17,33},{33,17},{49,1},{2,50}... | collective-permute-start | bytes 393224 | tf_op jit(solution)/shard_map/ppermute | solution.py:379
  227.1 5.3 %finish.1 = (bf16[1,128,2048]{2,1,0:T(8,128)(2,1)}, bf16[1,128,2048]{2,1,0:T(8,128)(2,1)}, bf16[1,128,2048]{2,1,0:T(8,128)(2,1)}) custom-call(s32[3]{0:T(128)S(1)} %pad_add_fusion.idx_ref, bf16[4,4,160,128]{3,2,1,0:T(8,128)(2,1)S(1)} %pad_maximum_fusion.3.x_ref, f32[128,2048]{1,0:T(8,128)S(1)} %copy-done.7, f32[16,8,128]{2,1,0:T(8,128)S(1)} %get-tuple-element.62.s_ref, ...), custom_call_target="tpu_custom_call" | custom-call | flops 335544320 | bytes 5242880 | tf_op jit(solution)/shard_map/finish/pallas_call | solution.py:323
  232.5 8.1 %collective-permute-done.36.refs_3_ = bf16[128,512]{1,0:T(8,128)(2,1)S(1)} collective-permute-done((bf16[128,512]{1,0:T(8,128)(2,1)S(1)}, bf16[128,512]{1,0:T(8,128)(2,1)S(1)}, u32[]{:S(2)}, u32[]{:S(2)}) %collective-permute-start.36) | collective-permute-done | bytes 131104 | tf_op jit(solution)/shard_map/ppermute | solution.py:379
  (152 shorter events, 54.5 us)
Async XLA Ops:
  6.1 13.1 %collective-permute-start.4 = (bf16[128,2048]{1,0:T(8,128)(2,1)}, bf16[128,2048]{1,0:T(8,128)(2,1)}, u32[]{:S(2)}, u32[]{:S(2)}) collective-permute-start(bf16[128,2048]{1,0:T(8,128)(2,1)} %bitcast.96), channel_id=1, source_target_pairs={{0,32},{16,48},{32,0},{48,16},{1,33},{17,49},{33,1},{49,17},{2,34}... | collective-permute-start | bytes 1572872 | tf_op jit(solution)/shard_map/ppermute | solution.py:379
  6.2 13.0 %collective-permute-start.3 = (bf16[128,2048]{1,0:T(8,128)(2,1)}, bf16[128,2048]{1,0:T(8,128)(2,1)S(1)}, u32[]{:S(2)}, u32[]{:S(2)}) collective-permute-start(bf16[128,2048]{1,0:T(8,128)(2,1)} %bitcast.97), channel_id=1, source_target_pairs={{0,16},{16,0},{32,48},{48,32},{1,17},{17,1},{33,49},{49,33},{2,18}... | collective-permute-start | bytes 1572872 | tf_op jit(solution)/shard_map/ppermute | solution.py:379
  19.2 16.4 %collective-permute-start.5 = (bf16[4,128,512]{2,1,0:T(8,128)(2,1)S(1)}, bf16[4,128,512]{2,1,0:T(8,128)(2,1)S(1)}, u32[]{:S(2)}, u32[]{:S(2)}) collective-permute-start(bf16[4,128,512]{2,1,0:T(8,128)(2,1)S(1)} %maximum_select_fusion.1), channel_id=1, source_target_pairs={{0,2},{2,0},{1,3},{3,1},{4,6},{6,4},{5,7},{7,5},{8,10},{10,8},{9,1... | collective-permute-start | bytes 1572872 | tf_op jit(solution)/shard_map/ppermute | solution.py:393
  19.6 25.5 %collective-permute-start.6 = (bf16[128,2048]{1,0:T(8,128)(2,1)}, bf16[128,2048]{1,0:T(8,128)(2,1)}, u32[]{:S(2)}, u32[]{:S(2)}) collective-permute-start(bf16[128,2048]{1,0:T(8,128)(2,1)} %collective-permute-done.4), channel_id=1, source_target_pairs={{0,16},{16,0},{32,48},{48,32},{1,17},{17,1},{33,49},{49,33},{2,18}... | collective-permute-start | bytes 1572872 | tf_op jit(solution)/shard_map/ppermute | solution.py:379
  25.5 56.6 %all-to-all-start = ((bf16[16,3,128,128]{3,2,1,0:T(8,128)(2,1)}), bf16[16,3,128,128]{3,2,1,0:T(8,128)(2,1)S(1)}, u32[]{:S(2)}, u32[]{:S(2)}) async-start(bf16[16,3,128,128]{3,2,1,0:T(8,128)(2,1)} %by_heads.1), calls=%async_computation | async-start | bytes 3145728 | tf_op jit(solution)/shard_map/all_to_all | solution.py:371
  53.2 20.9 %collective-permute-start.9 = (bf16[512,128]{1,0:T(8,128)(2,1)S(1)}, bf16[512,128]{1,0:T(8,128)(2,1)S(1)}, u32[]{:S(2)}, u32[]{:S(2)}) collective-permute-start(bf16[512,128]{1,0:T(8,128)(2,1)S(1)} %get-tuple-element.83), channel_id=1, source_target_pairs={{0,64},{64,128},{128,192},{192,0},{1,65},{65,129},{129,193},{193,1... | collective-permute-start | bytes 393224 | tf_op jit(solution)/shard_map/ppermute | solution.py:375
  55.5 19.6 %collective-permute-start.10 = (bf16[512,128]{1,0:T(8,128)(2,1)S(1)}, bf16[512,128]{1,0:T(8,128)(2,1)S(1)}, u32[]{:S(2)}, u32[]{:S(2)}) collective-permute-start(bf16[512,128]{1,0:T(8,128)(2,1)S(1)} %get-tuple-element.84), channel_id=1, source_target_pairs={{0,192},{64,0},{128,64},{192,128},{1,193},{65,1},{129,65},{193,129... | collective-permute-start | bytes 393224 | tf_op jit(solution)/shard_map/ppermute | solution.py:375
  61.4 20.7 %collective-permute-start.8 = (bf16[512,128]{1,0:T(8,128)(2,1)S(1)}, bf16[512,128]{1,0:T(8,128)(2,1)S(1)}, u32[]{:S(2)}, u32[]{:S(2)}) collective-permute-start(bf16[512,128]{1,0:T(8,128)(2,1)S(1)} %get-tuple-element.86), channel_id=1, source_target_pairs={{0,128},{64,192},{128,0},{192,64},{1,129},{65,193},{129,1},{193,65... | collective-permute-start | bytes 393224 | tf_op jit(solution)/shard_map/ppermute | solution.py:375
  82.1 16.7 %collective-permute-start.13 = (bf16[128,512]{1,0:T(8,128)(2,1)S(1)}, bf16[128,512]{1,0:T(8,128)(2,1)S(1)}, u32[]{:S(2)}, u32[]{:S(2)}) collective-permute-start(bf16[128,512]{1,0:T(8,128)(2,1)S(1)} %get-tuple-element.80), channel_id=1, source_target_pairs={{0,48},{16,32},{32,16},{48,0},{1,49},{17,33},{33,17},{49,1},{2,50}... | collective-permute-start | bytes 393224 | tf_op jit(solution)/shard_map/ppermute | solution.py:379
  83.0 15.9 %collective-permute-start.12 = (bf16[128,512]{1,0:T(8,128)(2,1)S(1)}, bf16[128,512]{1,0:T(8,128)(2,1)S(1)}, u32[]{:S(2)}, u32[]{:S(2)}) collective-permute-start(bf16[128,512]{1,0:T(8,128)(2,1)S(1)} %get-tuple-element.81), channel_id=1, source_target_pairs={{0,32},{16,48},{32,0},{48,16},{1,33},{17,49},{33,1},{49,17},{2,34}... | collective-permute-start | bytes 393224 | tf_op jit(solution)/shard_map/ppermute | solution.py:379
  85.2 13.7 %collective-permute-start.11 = (bf16[128,512]{1,0:T(8,128)(2,1)S(1)}, bf16[128,512]{1,0:T(8,128)(2,1)S(1)}, u32[]{:S(2)}, u32[]{:S(2)}) collective-permute-start(bf16[128,512]{1,0:T(8,128)(2,1)S(1)} %get-tuple-element.82), channel_id=1, source_target_pairs={{0,16},{16,0},{32,48},{48,32},{1,17},{17,1},{33,49},{49,33},{2,18}... | collective-permute-start | bytes 393224 | tf_op jit(solution)/shard_map/ppermute | solution.py:379
  94.7 21.7 %collective-permute-start.15 = (bf16[2,288,128]{2,1,0:T(8,128)(2,1)S(1)}, bf16[2,288,128]{2,1,0:T(8,128)(2,1)S(1)}, u32[]{:S(2)}, u32[]{:S(2)}) collective-permute-start(bf16[2,288,128]{2,1,0:T(8,128)(2,1)S(1)} %get-tuple-element.77), channel_id=1, source_target_pairs={{0,64},{64,128},{128,192},{192,0},{1,65},{65,129},{129,193},{193,1... | collective-permute-start | bytes 442376 | tf_op jit(solution)/shard_map/ppermute | solution.py:375
  94.8 21.6 %collective-permute-start.14 = (bf16[2,288,128]{2,1,0:T(8,128)(2,1)S(1)}, bf16[2,288,128]{2,1,0:T(8,128)(2,1)S(1)}, u32[]{:S(2)}, u32[]{:S(2)}) collective-permute-start(bf16[2,288,128]{2,1,0:T(8,128)(2,1)S(1)} %get-tuple-element.78), channel_id=1, source_target_pairs={{0,192},{64,0},{128,64},{192,128},{1,193},{65,1},{129,65},{193,129... | collective-permute-start | bytes 442376 | tf_op jit(solution)/shard_map/ppermute | solution.py:375
  112.9 36.2 %collective-permute-start.22 = (bf16[288,512]{1,0:T(8,128)(2,1)S(1)}, bf16[288,512]{1,0:T(8,128)(2,1)S(1)}, u32[]{:S(2)}, u32[]{:S(2)}) collective-permute-start(bf16[288,512]{1,0:T(8,128)(2,1)S(1)} %get-tuple-element.69), channel_id=1, source_target_pairs={{0,48},{16,32},{32,16},{48,0},{1,49},{17,33},{33,17},{49,1},{2,50}... | collective-permute-start | bytes 884744 | tf_op jit(solution)/shard_map/ppermute | solution.py:379
  113.9 35.2 %collective-permute-start.21 = (bf16[288,512]{1,0:T(8,128)(2,1)S(1)}, bf16[288,512]{1,0:T(8,128)(2,1)S(1)}, u32[]{:S(2)}, u32[]{:S(2)}) collective-permute-start(bf16[288,512]{1,0:T(8,128)(2,1)S(1)} %get-tuple-element.70), channel_id=1, source_target_pairs={{0,32},{16,48},{32,0},{48,16},{1,33},{17,49},{33,1},{49,17},{2,34}... | collective-permute-start | bytes 884744 | tf_op jit(solution)/shard_map/ppermute | solution.py:379
  115.9 33.2 %collective-permute-start.20 = (bf16[288,512]{1,0:T(8,128)(2,1)S(1)}, bf16[288,512]{1,0:T(8,128)(2,1)S(1)}, u32[]{:S(2)}, u32[]{:S(2)}) collective-permute-start(bf16[288,512]{1,0:T(8,128)(2,1)S(1)} %get-tuple-element.71), channel_id=1, source_target_pairs={{0,16},{16,0},{32,48},{48,32},{1,17},{17,1},{33,49},{49,33},{2,18}... | collective-permute-start | bytes 884744 | tf_op jit(solution)/shard_map/ppermute | solution.py:379
  125.0 13.2 %collective-permute-start.18 = (bf16[2,288,128]{2,1,0:T(8,128)(2,1)S(1)}, bf16[2,288,128]{2,1,0:T(8,128)(2,1)S(1)}, u32[]{:S(2)}, u32[]{:S(2)}) collective-permute-start(bf16[2,288,128]{2,1,0:T(8,128)(2,1)S(1)} %collective-permute-done.15), channel_id=1, source_target_pairs={{0,64},{64,128},{128,192},{192,0},{1,65},{65,129},{129,193},{193,1... | collective-permute-start | bytes 442376 | tf_op jit(solution)/shard_map/ppermute | solution.py:375
  132.6 16.5 %collective-permute-start.19 = (bf16[4,288,128]{2,1,0:T(8,128)(2,1)S(1)}, bf16[4,288,128]{2,1,0:T(8,128)(2,1)S(1)}, u32[]{:S(2)}, u32[]{:S(2)}) collective-permute-start(bf16[4,288,128]{2,1,0:T(8,128)(2,1)S(1)} %get-tuple-element.75), channel_id=1, source_target_pairs={{0,64},{64,128},{128,192},{192,0},{1,65},{65,129},{129,193},{193,1... | collective-permute-start | bytes 884744 | tf_op jit(solution)/shard_map/ppermute | solution.py:375
  138.2 17.7 %collective-permute-start.16 = (bf16[4,288,128]{2,1,0:T(8,128)(2,1)S(1)}, bf16[4,288,128]{2,1,0:T(8,128)(2,1)S(1)}, u32[]{:S(2)}, u32[]{:S(2)}) collective-permute-start(bf16[4,288,128]{2,1,0:T(8,128)(2,1)S(1)} %get-tuple-element.76), channel_id=1, source_target_pairs={{0,192},{64,0},{128,64},{192,128},{1,193},{65,1},{129,65},{193,129... | collective-permute-start | bytes 884744 | tf_op jit(solution)/shard_map/ppermute | solution.py:375
  161.2 35.5 %all-to-all-start.1 = ((bf16[16,128,512]{2,1,0:T(8,128)(2,1)}), bf16[16,128,512]{2,1,0:T(8,128)(2,1)}, u32[]{:S(2)}, u32[]{:S(2)}) async-start(bf16[16,128,512]{2,1,0:T(8,128)(2,1)} %bitcast.77), calls=%async_computation.1 | async-start | bytes 4194304 | tf_op jit(solution)/shard_map/all_to_all | solution.py:371
  171.7 45.1 %collective-permute-start.29 = (bf16[2,128,2048]{2,1,0:T(8,128)(2,1)S(1)}, bf16[2,128,2048]{2,1,0:T(8,128)(2,1)}, u32[]{:S(2)}, u32[]{:S(2)}) collective-permute-start(bf16[2,128,2048]{2,1,0:T(8,128)(2,1)S(1)} %slice_bitcast_fusion.1), channel_id=1, source_target_pairs={{0,16},{16,0},{32,48},{48,32},{1,17},{17,1},{33,49},{49,33},{2,18}... | collective-permute-start | bytes 3145736 | tf_op jit(solution)/shard_map/ppermute | solution.py:379
  174.7 26.4 %collective-permute-start.23 = (bf16[4,160,128]{2,1,0:T(8,128)(2,1)}, bf16[4,160,128]{2,1,0:T(8,128)(2,1)S(1)}, u32[]{:S(2)}, u32[]{:S(2)}) collective-permute-start(bf16[4,160,128]{2,1,0:T(8,128)(2,1)} %get-tuple-element.54), channel_id=1, source_target_pairs={{0,192},{64,0},{128,64},{192,128},{1,193},{65,1},{129,65},{193,129... | collective-permute-start | bytes 491528 | tf_op jit(solution)/shard_map/ppermute | solution.py:375
  176.4 28.5 %collective-permute-start.24 = (bf16[4,160,128]{2,1,0:T(8,128)(2,1)}, bf16[4,160,128]{2,1,0:T(8,128)(2,1)S(1)}, u32[]{:S(2)}, u32[]{:S(2)}) collective-permute-start(bf16[4,160,128]{2,1,0:T(8,128)(2,1)} %get-tuple-element.55), channel_id=1, source_target_pairs={{0,128},{64,192},{128,0},{192,64},{1,129},{65,193},{129,1},{193,65... | collective-permute-start | bytes 491528 | tf_op jit(solution)/shard_map/ppermute | solution.py:375
  180.9 24.4 %collective-permute-start.25 = (bf16[4,160,128]{2,1,0:T(8,128)(2,1)}, bf16[4,160,128]{2,1,0:T(8,128)(2,1)S(1)}, u32[]{:S(2)}, u32[]{:S(2)}) collective-permute-start(bf16[4,160,128]{2,1,0:T(8,128)(2,1)} %get-tuple-element.56), channel_id=1, source_target_pairs={{0,64},{64,128},{128,192},{192,0},{1,65},{65,129},{129,193},{193,1... | collective-permute-start | bytes 491528 | tf_op jit(solution)/shard_map/ppermute | solution.py:375
  198.7 20.2 %collective-permute-start.33 = (bf16[128,512]{1,0:T(8,128)(2,1)S(1)}, bf16[128,512]{1,0:T(8,128)(2,1)S(1)}, u32[]{:S(2)}, u32[]{:S(2)}) collective-permute-start(bf16[128,512]{1,0:T(8,128)(2,1)S(1)} %reduce_sum.12), channel_id=1, source_target_pairs={{0,192},{64,0},{128,64},{192,128},{1,193},{65,1},{129,65},{193,129... | collective-permute-start | bytes 393224 | tf_op jit(solution)/shard_map/ppermute | solution.py:375
  201.1 20.1 %collective-permute-start.32 = (bf16[128,512]{1,0:T(8,128)(2,1)S(1)}, bf16[128,512]{1,0:T(8,128)(2,1)S(1)}, u32[]{:S(2)}, u32[]{:S(2)}) collective-permute-start(bf16[128,512]{1,0:T(8,128)(2,1)S(1)} %reduce_sum.12), channel_id=1, source_target_pairs={{0,128},{64,192},{128,0},{192,64},{1,129},{65,193},{129,1},{193,65... | collective-permute-start | bytes 393224 | tf_op jit(solution)/shard_map/ppermute | solution.py:375
  204.9 15.5 %collective-permute-start.31 = (bf16[128,512]{1,0:T(8,128)(2,1)S(1)}, bf16[128,512]{1,0:T(8,128)(2,1)S(1)}, u32[]{:S(2)}, u32[]{:S(2)}) collective-permute-start(bf16[128,512]{1,0:T(8,128)(2,1)S(1)} %reduce_sum.12), channel_id=1, source_target_pairs={{0,64},{64,128},{128,192},{192,0},{1,65},{65,129},{129,193},{193,1... | collective-permute-start | bytes 393224 | tf_op jit(solution)/shard_map/ppermute | solution.py:375
  205.4 18.8 %collective-permute-start.26 = (bf16[4,160,128]{2,1,0:T(8,128)(2,1)S(1)}, bf16[4,160,128]{2,1,0:T(8,128)(2,1)S(1)}, u32[]{:S(2)}, u32[]{:S(2)}) collective-permute-start(bf16[4,160,128]{2,1,0:T(8,128)(2,1)S(1)} %pad_maximum_fusion.10), channel_id=1, source_target_pairs={{0,16},{16,0},{32,48},{48,32},{1,17},{17,1},{33,49},{49,33},{2,18}... | collective-permute-start | bytes 491528 | tf_op jit(solution)/shard_map/ppermute | solution.py:379
  220.4 25.6 %collective-permute-start.30 = (bf16[128,2048]{1,0:T(8,128)(2,1)S(1)}, bf16[128,2048]{1,0:T(8,128)(2,1)S(1)}, u32[]{:S(2)}, u32[]{:S(2)}) collective-permute-start(bf16[128,2048]{1,0:T(8,128)(2,1)S(1)} %fusion.3), channel_id=1, source_target_pairs={{0,32},{16,48},{32,0},{48,16},{1,33},{17,49},{33,1},{49,17},{2,34}... | collective-permute-start | bytes 1572872 | tf_op jit(solution)/shard_map/ppermute | solution.py:379
  221.3 19.3 %collective-permute-start.36 = (bf16[128,512]{1,0:T(8,128)(2,1)S(1)}, bf16[128,512]{1,0:T(8,128)(2,1)S(1)}, u32[]{:S(2)}, u32[]{:S(2)}) collective-permute-start(bf16[128,512]{1,0:T(8,128)(2,1)S(1)} %add_convert_fusion.refs_0_), channel_id=1, source_target_pairs={{0,48},{16,32},{32,16},{48,0},{1,49},{17,33},{33,17},{49,1},{2,50}... | collective-permute-start | bytes 393224 | tf_op jit(solution)/shard_map/ppermute | solution.py:379
  224.3 18.2 %collective-permute-start.35 = (bf16[128,512]{1,0:T(8,128)(2,1)S(1)}, bf16[128,512]{1,0:T(8,128)(2,1)S(1)}, u32[]{:S(2)}, u32[]{:S(2)}) collective-permute-start(bf16[128,512]{1,0:T(8,128)(2,1)S(1)} %add_convert_fusion.refs_0_), channel_id=1, source_target_pairs={{0,32},{16,48},{32,0},{48,16},{1,33},{17,49},{33,1},{49,17},{2,34}... | collective-permute-start | bytes 393224 | tf_op jit(solution)/shard_map/ppermute | solution.py:379
  224.3 18.2 %collective-permute-start.34 = (bf16[128,512]{1,0:T(8,128)(2,1)S(1)}, bf16[128,512]{1,0:T(8,128)(2,1)S(1)}, u32[]{:S(2)}, u32[]{:S(2)}) collective-permute-start(bf16[128,512]{1,0:T(8,128)(2,1)S(1)} %add_convert_fusion.refs_0_), channel_id=1, source_target_pairs={{0,16},{16,0},{32,48},{48,32},{1,17},{17,1},{33,49},{49,33},{2,18}... | collective-permute-start | bytes 393224 | tf_op jit(solution)/shard_map/ppermute | solution.py:379
  (33 other events, 453.3 us)
where the time goes:
time: 253 us; the launch traced here: 248 us
  waiting for transfers between devices  96 us (38%)
  starting transfers between devices  83.1 us (33%)
  Pallas kernels  41.1 us (16%)
  matrix products  9.25 us (4%)
  other arithmetic  8.52 us (3%)
  local copies, waits for them, and re-layouts  8.2 us (3%)
    ppermute x18, starting transfers between devices, shift(): lax.ppermute(x, axis, [(s, (s + k) % 4) for s in range(4)])  46 us
    ppermute x18, waiting for transfers between devices, shift(): lax.ppermute(x, axis, [(s, (s + k) % 4) for s in range(4)])  40.7 us
    ppermute x17, waiting for transfers between devices, swap(): return lax.ppermute(x, axis, [(s, s ^ k) for s in range(4)]) if k else x  36 us
    ppermute x17, starting transfers between devices, swap(): return lax.ppermute(x, axis, [(s, s ^ k) for s in range(4)]) if k else x  20.9 us
    pallas_call x2, Pallas kernels, cross_attention(): pl.pallas_call(functools.partial(cross_kernel, slots=slots), grid_spec=pl...  17.1 us
    all_to_all x2, starting transfers between devices, a2a(): return lax.all_to_all(x, axis, 0, 0, tiled=True)  16 us
    all_to_all x2, waiting for transfers between devices, a2a(): return lax.all_to_all(x, axis, 0, 0, tiled=True)  15.9 us
    pallas_call x1, Pallas kernels, own_attention(): pl.pallas_call(own_kernel, grid_spec=pltpu.PrefetchScalarGridSpec(num_sca...  11.3 us
  transfers between devices with their start and end apart: 39, of which 18 were waited for; matrix products, arithmetic and copies ran while one was open for 6% of the time, Pallas kernels for 16%

commit v1 on v0

--- a/solution.py
+++ b/solution.py
@@ -383,12 +383,12 @@
     return jnp.stack([jnp.where(first, mine, other), jnp.where(first, other, mine)], axis=axis)
 
 
-def gather_shards(shard, tok1, tok2):
+def gather_shards(shard, tok1, tok2, kvg):
     x_index = lax.axis_index("x")
     slots = jnp.stack([shift(shard, "x", -k) for k in range(4)])
     slots = jnp.where(x_index % 2 == 1, jnp.roll(slots, 1, axis=0), slots)
     slots = jnp.where(x_index >= 2, jnp.roll(slots, 2, axis=0), slots)
-    slots, tok1, tok2 = lax.optimization_barrier((slots, tok1, tok2))
+    slots, tok1, tok2, _ = lax.optimization_barrier((slots, tok1, tok2, kvg))
     tok3 = swap(tok2, "q", 1)
     other = lax.ppermute(slots, "yh", [(0, 1), (1, 0)])
     slots = in_order(slots, other, lax.axis_index("yh") == 0, 1)
@@ -415,8 +415,8 @@
     idx = jnp.stack([g_index, q_index, cache_fill[0]]).astype(jnp.int32)
 
     own_tok = tokens[0]
+    kvg = by_heads(current_keys, current_values, attended_grad)
     tok2, tok1 = swap(own_tok, "q", 2), swap(own_tok, "q", 1)
-    kvg = by_heads(current_keys, current_values, attended_grad)
     quarter = jnp.concatenate(
         [
             lax.dynamic_slice_in_dim(
@@ -426,7 +426,7 @@
         ],
         axis=1,
     )
-    weight, tok1, tok2, tok3 = gather_shards(quarter, tok1, tok2)
+    weight, tok1, tok2, tok3 = gather_shards(quarter, tok1, tok2, kvg)
 
     kvg = a2a(kvg, XB)
 
@@ -473,12 +473,6 @@
     pieces = a2a(partial.reshape(16, query_weight.shape[0], 4 * HEAD), FS)
     mine = jnp.sum(pieces.astype(F32), axis=0).astype(BF)
 
-    part = dot_nt(qg, weight).astype(BF).reshape(2, 2, SEQ, -1)
-    swapped, _ = lax.optimization_barrier((swap(part[:, 1], "q", 1), mine))
-    near = part[:, 0].astype(F32) + swapped.astype(F32)
-    tokens_grad = near[0] + swap(near[1].astype(BF), "q", 2).astype(F32)
-    tokens_grad = tokens_grad.astype(BF)[None]
-
     out, _ = lax.optimization_barrier((out, partial))
     over_g = [shift(out[j], "g", -j) for j in range(4)]
     over_g, _ = lax.optimization_barrier((over_g, mine))
@@ -492,6 +486,13 @@
     summed = sum(
         jnp.roll(shift(mine, "g", k), -k * HEAD, axis=1).astype(F32) for k in range(4)
     ).astype(BF)
+
+    part = dot_nt(qg, weight).astype(BF).reshape(2, 2, SEQ, -1)
+    swapped, _ = lax.optimization_barrier((swap(part[:, 1], "q", 1), summed))
+    near = part[:, 0].astype(F32) + swapped.astype(F32)
+    tokens_grad = near[0] + swap(near[1].astype(BF), "q", 2).astype(F32)
+    tokens_grad = tokens_grad.astype(BF)[None]
+
     weight_grad = place(idx, [swap(summed, "q", k) for k in range(4)])
     return attended, tokens_grad, keys_grad, values_grad, weight_grad
 

time: 253 us -> 257 us (1.016)
  starting transfers between devices: 83.1 us -> 92.8 us
  waiting for transfers between devices: 96 us -> 89 us
    ppermute x18, starting transfers between devices: 46 us -> 54.6 us  [shift(): lax.ppermute(x, axis, [(s, (s + k) % 4) for s in range(4)])]
    ppermute x18, waiting for transfers between devices: 40.7 us -> 35.4 us  [shift(): lax.ppermute(x, axis, [(s, (s + k) % 4) for s in range(4)])]
    ppermute x17, waiting for transfers between devices: 36 us -> 30.8 us  [swap(): return lax.ppermute(x, axis, [(s, s ^ k) for s in range(4)]) if k else x]
    ppermute x1, waiting for transfers between devices: 0.89 us -> 4.61 us  [gather_shards(): other = lax.ppermute(slots, 'yh', [(0, 1), (1, 0)])]
    all_to_all x2, starting transfers between devices: 16 us -> 18.9 us  [a2a(): return lax.all_to_all(x, axis, 0, 0, tiled=True)]
    unnamed x52 -> x54, local copies, waits for them, and re-layouts: 5.02 us -> 6.34 us
  transfers between devices with their start and end apart: 39 -> 39, of which waited for: 18 -> 17; matrix products, arithmetic and copies ran while one was open for 6% -> 6% of each run, Pallas kernels for 16% -> 16%
where the time goes in v1:
time: 257 us; the launch traced here: 253 us
  starting transfers between devices  92.8 us (36%)
  waiting for transfers between devices  89 us (35%)
  Pallas kernels  41.1 us (16%)
  local copies, waits for them, and re-layouts  10.4 us (4%)
  matrix products  9.24 us (4%)
  other arithmetic  8.22 us (3%)
    ppermute x18, starting transfers between devices, shift(): lax.ppermute(x, axis, [(s, (s + k) % 4) for s in range(4)])  54.6 us
    ppermute x18, waiting for transfers between devices, shift(): lax.ppermute(x, axis, [(s, (s + k) % 4) for s in range(4)])  35.4 us
    ppermute x17, waiting for transfers between devices, swap(): return lax.ppermute(x, axis, [(s, s ^ k) for s in range(4)]) if k else x  30.8 us
    all_to_all x2, starting transfers between devices, a2a(): return lax.all_to_all(x, axis, 0, 0, tiled=True)  18.9 us
    ppermute x17, starting transfers between devices, swap(): return lax.ppermute(x, axis, [(s, s ^ k) for s in range(4)]) if k else x  18.9 us
    pallas_call x2, Pallas kernels, cross_attention(): pl.pallas_call(functools.partial(cross_kernel, slots=slots), grid_spec=pl...  17.1 us
    all_to_all x2, waiting for transfers between devices, a2a(): return lax.all_to_all(x, axis, 0, 0, tiled=True)  15.7 us
    pallas_call x1, Pallas kernels, own_attention(): pl.pallas_call(own_kernel, grid_spec=pltpu.PrefetchScalarGridSpec(num_sca...  11.3 us
  transfers between devices with their start and end apart: 39, of which 17 were waited for; matrix products, arithmetic and copies ran while one was open for 6% of the time, Pallas kernels for 16%

profile of v1, /device:TPU:48, one launch (start us, length us, event | category | flops | bytes accessed | tf_op | source)
XLA Modules:
  0.0 253.0 jit_solution(14540094849524730854)
XLA Ops:
  1.6 2.8 %collective-permute-start.1 = (bf16[128,512]{1,0:T(8,128)(2,1)S(1)}, bf16[128,512]{1,0:T(8,128)(2,1)S(1)}, u32[]{:S(2)}, u32[]{:S(2)}) collective-permute-start(bf16[128,512]{1,0:T(8,128)(2,1)S(1)} %get-tuple-element.116), channel_id=1, source_target_pairs={{0,12},{4,0},{8,4},{12,8},{1,13},{5,1},{9,5},{13,9},{2,14},{6,2},{... | collective-permute-start | bytes 393224 | tf_op jit(solution)/shard_map/ppermute | solution.py:375
  7.5 3.7 %by_heads.1 = bf16[16,3,128,128]{3,2,1,0:T(8,128)(2,1)} custom-call(bf16[1,128,2048]{2,1,0:T(8,128)(2,1)} %lk_ref.3, bf16[1,128,2048]{2,1,0:T(8,128)(2,1)} %lv_ref.3, bf16[1,128,2048]{2,1,0:T(8,128)(2,1)} %g_ref.3), custom_call_target="tpu_custom_call" | custom-call | bytes 3145728 | tf_op jit(solution)/shard_map/by_heads/pallas_call | solution.py:151
  14.0 5.2 %collective-permute-done.4 = bf16[128,2048]{1,0:T(8,128)(2,1)} collective-permute-done((bf16[128,2048]{1,0:T(8,128)(2,1)}, bf16[128,2048]{1,0:T(8,128)(2,1)}, u32[]{:S(2)}, u32[]{:S(2)}) %collective-permute-start.4) | collective-permute-done | bytes 524320 | tf_op jit(solution)/shard_map/ppermute | solution.py:379
  21.7 9.2 %all-to-all-start = ((bf16[16,3,128,128]{3,2,1,0:T(8,128)(2,1)}), bf16[16,3,128,128]{3,2,1,0:T(8,128)(2,1)S(1)}, u32[]{:S(2)}, u32[]{:S(2)}) async-start(bf16[16,3,128,128]{3,2,1,0:T(8,128)(2,1)} %by_heads.1), calls=%async_computation | async-start | bytes 3145728 | tf_op jit(solution)/shard_map/all_to_all | solution.py:371
  31.0 4.6 %collective-permute-done.5 = bf16[4,128,512]{2,1,0:T(8,128)(2,1)S(1)} collective-permute-done((bf16[4,128,512]{2,1,0:T(8,128)(2,1)S(1)}, bf16[4,128,512]{2,1,0:T(8,128)(2,1)S(1)}, u32[]{:S(2)}, u32[]{:S(2)}) %collective-permute-start.5) | collective-permute-done | bytes 524320 | tf_op jit(solution)/shard_map/ppermute | solution.py:393
  35.8 10.1 %collective-permute-done.6 = bf16[128,2048]{1,0:T(8,128)(2,1)} collective-permute-done((bf16[128,2048]{1,0:T(8,128)(2,1)}, bf16[128,2048]{1,0:T(8,128)(2,1)}, u32[]{:S(2)}, u32[]{:S(2)}) %collective-permute-start.6) | collective-permute-done | bytes 524320 | tf_op jit(solution)/shard_map/ppermute | solution.py:379
  46.1 2.5 collective-permute-done.7
  54.0 3.6 %collective-permute-start.9 = (bf16[512,128]{1,0:T(8,128)(2,1)S(1)}, bf16[512,128]{1,0:T(8,128)(2,1)S(1)}, u32[]{:S(2)}, u32[]{:S(2)}) collective-permute-start(bf16[512,128]{1,0:T(8,128)(2,1)S(1)} %get-tuple-element.83), channel_id=1, source_target_pairs={{0,64},{64,128},{128,192},{192,0},{1,65},{65,129},{129,193},{193,1... | collective-permute-start | bytes 393224 | tf_op jit(solution)/shard_map/ppermute | solution.py:375
  57.6 5.8 %collective-permute-start.10 = (bf16[512,128]{1,0:T(8,128)(2,1)S(1)}, bf16[512,128]{1,0:T(8,128)(2,1)S(1)}, u32[]{:S(2)}, u32[]{:S(2)}) collective-permute-start(bf16[512,128]{1,0:T(8,128)(2,1)S(1)} %get-tuple-element.84), channel_id=1, source_target_pairs={{0,192},{64,0},{128,64},{192,128},{1,193},{65,1},{129,65},{193,129... | collective-permute-start | bytes 393224 | tf_op jit(solution)/shard_map/ppermute | solution.py:375
  64.1 4.7 %collective-permute-start.8 = (bf16[512,128]{1,0:T(8,128)(2,1)S(1)}, bf16[512,128]{1,0:T(8,128)(2,1)S(1)}, u32[]{:S(2)}, u32[]{:S(2)}) collective-permute-start(bf16[512,128]{1,0:T(8,128)(2,1)S(1)} %get-tuple-element.86), channel_id=1, source_target_pairs={{0,128},{64,192},{128,0},{192,64},{1,129},{65,193},{129,1},{193,65... | collective-permute-start | bytes 393224 | tf_op jit(solution)/shard_map/ppermute | solution.py:375
  71.5 6.7 %collective-permute-done.8 = bf16[512,128]{1,0:T(8,128)(2,1)S(1)} collective-permute-done((bf16[512,128]{1,0:T(8,128)(2,1)S(1)}, bf16[512,128]{1,0:T(8,128)(2,1)S(1)}, u32[]{:S(2)}, u32[]{:S(2)}) %collective-permute-start.8) | collective-permute-done | bytes 131104 | tf_op jit(solution)/shard_map/ppermute | solution.py:375
  82.3 8.6 %cross.2 = (bf16[8,288,128]{2,1,0:T(8,128)(2,1)S(1)}, bf16[8,160,128]{2,1,0:T(8,128)(2,1)S(1)}) custom-call(s32[3]{0:T(128)S(1)} %pad_add_fusion.idx_ref, bf16[8,128,128]{2,1,0:T(8,128)(2,1)S(1)} %pad_maximum_fusion.8.q_ref, bf16[16,3,128,128]{3,2,1,0:T(8,128)(2,1)S(1)} %all-to-all-done.kvg_ref, f32[16,1,2048]{2,1,0:T(1,128)S(1)} %bitcast.73), custom_call_target="tpu_custom_call" | custom-call | flops 131072 | bytes 65536 | tf_op jit(solution)/shard_map/cross/pallas_call | solution.py:110
  91.0 4.1 %collective-permute-start.14 = (bf16[2,288,128]{2,1,0:T(8,128)(2,1)S(1)}, bf16[2,288,128]{2,1,0:T(8,128)(2,1)S(1)}, u32[]{:S(2)}, u32[]{:S(2)}) collective-permute-start(bf16[2,288,128]{2,1,0:T(8,128)(2,1)S(1)} %get-tuple-element.78), channel_id=1, source_target_pairs={{0,192},{64,0},{128,64},{192,128},{1,193},{65,1},{129,65},{193,129... | collective-permute-start | bytes 442376 | tf_op jit(solution)/shard_map/ppermute | solution.py:375
  96.8 11.3 %own.1 = (bf16[4,288,512]{2,1,0:T(8,128)(2,1)S(1)}, f32[128,2048]{1,0:T(8,128)S(1)}, f32[16,8,128]{2,1,0:T(8,128)S(1)}) custom-call(s32[3]{0:T(128)S(1)} %pad_add_fusion.idx_ref, bf16[4,128,512]{2,1,0:T(8,128)(2,1)S(1)} %pad_maximum_fusion.4.q_ref, bf16[1,128,2048]{2,1,0:T(8,128)(2,1)S(1)} %copy-done.2, bf16[1,512,2048]{2,1,0:T(8,128)(2,1)S(1)} %copy-done.4, ...), custom_call_target="tpu_custom_call" | custom-call | flops 65536 | bytes 65536 | tf_op jit(solution)/shard_map/own/pallas_call | solution.py:206
  112.6 8.6 %cross.3 = (bf16[8,288,128]{2,1,0:T(8,128)(2,1)S(1)}, bf16[8,160,128]{2,1,0:T(8,128)(2,1)S(1)}) custom-call(s32[3]{0:T(128)S(1)} %pad_add_fusion.idx_ref, bf16[8,128,128]{2,1,0:T(8,128)(2,1)S(1)} %pad_maximum_fusion.9.q_ref, bf16[16,3,128,128]{3,2,1,0:T(8,128)(2,1)S(1)} %all-to-all-done.kvg_ref, f32[16,1,2048]{2,1,0:T(1,128)S(1)} %bitcast.74), custom_call_target="tpu_custom_call" | custom-call | flops 131072 | bytes 65536 | tf_op jit(solution)/shard_map/cross/pallas_call | solution.py:110
  121.3 2.9 %collective-permute-start.18 = (bf16[2,288,128]{2,1,0:T(8,128)(2,1)S(1)}, bf16[2,288,128]{2,1,0:T(8,128)(2,1)S(1)}, u32[]{:S(2)}, u32[]{:S(2)}) collective-permute-start(bf16[2,288,128]{2,1,0:T(8,128)(2,1)S(1)} %collective-permute-done.15), channel_id=1, source_target_pairs={{0,64},{64,128},{128,192},{192,0},{1,65},{65,129},{129,193},{193,1... | collective-permute-start | bytes 442376 | tf_op jit(solution)/shard_map/ppermute | solution.py:375
  124.3 3.7 %collective-permute-done.17 = bf16[2,288,128]{2,1,0:T(8,128)(2,1)S(1)} collective-permute-done((bf16[2,288,128]{2,1,0:T(8,128)(2,1)S(1)}, bf16[2,288,128]{2,1,0:T(8,128)(2,1)S(1)}, u32[]{:S(2)}, u32[]{:S(2)}) %collective-permute-start.17) | collective-permute-done | bytes 147488 | tf_op jit(solution)/shard_map/ppermute | solution.py:375
  128.0 2.9 %collective-permute-start.19 = (bf16[4,288,128]{2,1,0:T(8,128)(2,1)S(1)}, bf16[4,288,128]{2,1,0:T(8,128)(2,1)S(1)}, u32[]{:S(2)}, u32[]{:S(2)}) collective-permute-start(bf16[4,288,128]{2,1,0:T(8,128)(2,1)S(1)} %get-tuple-element.75), channel_id=1, source_target_pairs={{0,64},{64,128},{128,192},{192,0},{1,65},{65,129},{129,193},{193,1... | collective-permute-start | bytes 884744 | tf_op jit(solution)/shard_map/ppermute | solution.py:375
  130.8 11.4 %collective-permute-start.16 = (bf16[4,288,128]{2,1,0:T(8,128)(2,1)S(1)}, bf16[4,288,128]{2,1,0:T(8,128)(2,1)S(1)}, u32[]{:S(2)}, u32[]{:S(2)}) collective-permute-start(bf16[4,288,128]{2,1,0:T(8,128)(2,1)S(1)} %get-tuple-element.76), channel_id=1, source_target_pairs={{0,192},{64,0},{128,64},{192,128},{1,193},{65,1},{129,65},{193,129... | collective-permute-start | bytes 884744 | tf_op jit(solution)/shard_map/ppermute | solution.py:375
  143.0 9.1 %collective-permute-done.16.refs_1_ = bf16[4,288,128]{2,1,0:T(8,128)(2,1)S(1)} collective-permute-done((bf16[4,288,128]{2,1,0:T(8,128)(2,1)S(1)}, bf16[4,288,128]{2,1,0:T(8,128)(2,1)S(1)}, u32[]{:S(2)}, u32[]{:S(2)}) %collective-permute-start.16) | collective-permute-done | bytes 294944 | tf_op jit(solution)/shard_map/ppermute | solution.py:375
  153.6 3.9 %convolution_convert_fusion.1 = bf16[2048,512]{1,0:T(8,128)(2,1)} fusion(bf16[512,512]{1,0:T(8,128)(2,1)S(1)} %dest.1, bf16[128,2048]{1,0:T(8,128)(2,1)} %collective-permute-done.6, bf16[128,2048]{1,0:T(8,128)(2,1)} %collective-permute-done.4, bf16[128,2048]{1,0:T(8,128)(2,1)S(1)} %copy-done.26, bf16[128,2048]{1,0:T(8,128)(2,1)S(1)} %bitcast.99), kind=kOutput, calls=%fused_computation.1 | convolution fusion | flops 1083179008 | bytes 4718592 | tf_op jit(solution)/shard_map/dot_general | solution.py:470
  157.5 9.7 %all-to-all-start.1 = ((bf16[16,128,512]{2,1,0:T(8,128)(2,1)}), bf16[16,128,512]{2,1,0:T(8,128)(2,1)}, u32[]{:S(2)}, u32[]{:S(2)}) async-start(bf16[16,128,512]{2,1,0:T(8,128)(2,1)} %bitcast.77), calls=%async_computation.1 | async-start | bytes 4194304 | tf_op jit(solution)/shard_map/all_to_all | solution.py:371
  168.7 3.7 %collective-permute-start.23 = (bf16[4,160,128]{2,1,0:T(8,128)(2,1)}, bf16[4,160,128]{2,1,0:T(8,128)(2,1)}, u32[]{:S(2)}, u32[]{:S(2)}) collective-permute-start(bf16[4,160,128]{2,1,0:T(8,128)(2,1)} %get-tuple-element.54), channel_id=1, source_target_pairs={{0,192},{64,0},{128,64},{192,128},{1,193},{65,1},{129,65},{193,129... | collective-permute-start | bytes 491528 | tf_op jit(solution)/shard_map/ppermute | solution.py:375
  172.3 3.5 %collective-permute-start.24 = (bf16[4,160,128]{2,1,0:T(8,128)(2,1)}, bf16[4,160,128]{2,1,0:T(8,128)(2,1)S(1)}, u32[]{:S(2)}, u32[]{:S(2)}) collective-permute-start(bf16[4,160,128]{2,1,0:T(8,128)(2,1)} %get-tuple-element.55), channel_id=1, source_target_pairs={{0,128},{64,192},{128,0},{192,64},{1,129},{65,193},{129,1},{193,65... | collective-permute-start | bytes 491528 | tf_op jit(solution)/shard_map/ppermute | solution.py:375
  175.9 2.9 %convolution_convert_fusion = bf16[512,2048]{1,0:T(8,128)(2,1)S(1)} fusion(bf16[512,512]{1,0:T(8,128)(2,1)S(1)} %dest.1, bf16[2048,512]{1,0:T(8,128)(2,1)} %bitcast.76), kind=kOutput, calls=%fused_computation | convolution fusion | flops 1074790400 | bytes 4718592 | tf_op jit(solution)/shard_map/dot_general | solution.py:25
  180.3 15.7 %all-to-all-done.1 = bf16[16,128,512]{2,1,0:T(8,128)(2,1)} async-done(((bf16[16,128,512]{2,1,0:T(8,128)(2,1)}), bf16[16,128,512]{2,1,0:T(8,128)(2,1)}, u32[]{:S(2)}, u32[]{:S(2)}) %all-to-all-start.1) | async-done | bytes 2097184 | tf_op jit(solution)/shard_map/all_to_all | solution.py:371
  198.0 3.8 %collective-permute-start.32 = (bf16[128,512]{1,0:T(8,128)(2,1)S(1)}, bf16[128,512]{1,0:T(8,128)(2,1)S(1)}, u32[]{:S(2)}, u32[]{:S(2)}) collective-permute-start(bf16[128,512]{1,0:T(8,128)(2,1)S(1)} %reduce_sum.12), channel_id=1, source_target_pairs={{0,192},{64,0},{128,64},{192,128},{1,193},{65,1},{129,65},{193,129... | collective-permute-start | bytes 393224 | tf_op jit(solution)/shard_map/ppermute | solution.py:375
  201.7 3.5 %collective-permute-start.31 = (bf16[128,512]{1,0:T(8,128)(2,1)S(1)}, bf16[128,512]{1,0:T(8,128)(2,1)S(1)}, u32[]{:S(2)}, u32[]{:S(2)}) collective-permute-start(bf16[128,512]{1,0:T(8,128)(2,1)S(1)} %reduce_sum.12), channel_id=1, source_target_pairs={{0,128},{64,192},{128,0},{192,64},{1,129},{65,193},{129,1},{193,65... | collective-permute-start | bytes 393224 | tf_op jit(solution)/shard_map/ppermute | solution.py:375
  208.3 8.0 %collective-permute-done.30 = bf16[128,512]{1,0:T(8,128)(2,1)S(1)} collective-permute-done((bf16[128,512]{1,0:T(8,128)(2,1)S(1)}, bf16[128,512]{1,0:T(8,128)(2,1)S(1)}, u32[]{:S(2)}, u32[]{:S(2)}) %collective-permute-start.30) | collective-permute-done | bytes 131104 | tf_op jit(solution)/shard_map/ppermute | solution.py:375
  224.2 12.4 %collective-permute-done.27 = bf16[4,160,128]{2,1,0:T(8,128)(2,1)S(1)} collective-permute-done((bf16[4,160,128]{2,1,0:T(8,128)(2,1)S(1)}, bf16[4,160,128]{2,1,0:T(8,128)(2,1)S(1)}, u32[]{:S(2)}, u32[]{:S(2)}) %collective-permute-start.27) | collective-permute-done | bytes 163872 | tf_op jit(solution)/shard_map/ppermute | solution.py:379
  238.6 3.0 %collective-permute-done.28 = bf16[4,160,128]{2,1,0:T(8,128)(2,1)S(1)} collective-permute-done((bf16[4,160,128]{2,1,0:T(8,128)(2,1)S(1)}, bf16[4,160,128]{2,1,0:T(8,128)(2,1)S(1)}, u32[]{:S(2)}, u32[]{:S(2)}) %collective-permute-start.28) | collective-permute-done | bytes 163872 | tf_op jit(solution)/shard_map/ppermute | solution.py:379
  241.7 5.3 %finish.1 = (bf16[1,128,2048]{2,1,0:T(8,128)(2,1)}, bf16[1,128,2048]{2,1,0:T(8,128)(2,1)}, bf16[1,128,2048]{2,1,0:T(8,128)(2,1)}) custom-call(s32[3]{0:T(128)S(1)} %pad_add_fusion.idx_ref, bf16[4,4,160,128]{3,2,1,0:T(8,128)(2,1)S(1)} %pad_maximum_fusion.3.x_ref, f32[128,2048]{1,0:T(8,128)S(1)} %copy-done.7, f32[16,8,128]{2,1,0:T(8,128)S(1)} %get-tuple-element.62.s_ref, ...), custom_call_target="tpu_custom_call" | custom-call | flops 335544320 | bytes 5242880 | tf_op jit(solution)/shard_map/finish/pallas_call | solution.py:323
  (154 shorter events, 53.6 us)
Async XLA Ops:
  6.1 13.1 %collective-permute-start.4 = (bf16[128,2048]{1,0:T(8,128)(2,1)}, bf16[128,2048]{1,0:T(8,128)(2,1)}, u32[]{:S(2)}, u32[]{:S(2)}) collective-permute-start(bf16[128,2048]{1,0:T(8,128)(2,1)} %bitcast.96), channel_id=1, source_target_pairs={{0,32},{16,48},{32,0},{48,16},{1,33},{17,49},{33,1},{49,17},{2,34}... | collective-permute-start | bytes 1572872 | tf_op jit(solution)/shard_map/ppermute | solution.py:379
  6.2 13.0 %collective-permute-start.3 = (bf16[128,2048]{1,0:T(8,128)(2,1)}, bf16[128,2048]{1,0:T(8,128)(2,1)S(1)}, u32[]{:S(2)}, u32[]{:S(2)}) collective-permute-start(bf16[128,2048]{1,0:T(8,128)(2,1)} %bitcast.97), channel_id=1, source_target_pairs={{0,16},{16,0},{32,48},{48,32},{1,17},{17,1},{33,49},{49,33},{2,18}... | collective-permute-start | bytes 1572872 | tf_op jit(solution)/shard_map/ppermute | solution.py:379
  19.2 16.4 %collective-permute-start.5 = (bf16[4,128,512]{2,1,0:T(8,128)(2,1)S(1)}, bf16[4,128,512]{2,1,0:T(8,128)(2,1)S(1)}, u32[]{:S(2)}, u32[]{:S(2)}) collective-permute-start(bf16[4,128,512]{2,1,0:T(8,128)(2,1)S(1)} %maximum_select_fusion.1), channel_id=1, source_target_pairs={{0,2},{2,0},{1,3},{3,1},{4,6},{6,4},{5,7},{7,5},{8,10},{10,8},{9,1... | collective-permute-start | bytes 1572872 | tf_op jit(solution)/shard_map/ppermute | solution.py:393
  19.6 26.3 %collective-permute-start.6 = (bf16[128,2048]{1,0:T(8,128)(2,1)}, bf16[128,2048]{1,0:T(8,128)(2,1)}, u32[]{:S(2)}, u32[]{:S(2)}) collective-permute-start(bf16[128,2048]{1,0:T(8,128)(2,1)} %collective-permute-done.4), channel_id=1, source_target_pairs={{0,16},{16,0},{32,48},{48,32},{1,17},{17,1},{33,49},{49,33},{2,18}... | collective-permute-start | bytes 1572872 | tf_op jit(solution)/shard_map/ppermute | solution.py:379
  21.7 56.5 %all-to-all-start = ((bf16[16,3,128,128]{3,2,1,0:T(8,128)(2,1)}), bf16[16,3,128,128]{3,2,1,0:T(8,128)(2,1)S(1)}, u32[]{:S(2)}, u32[]{:S(2)}) async-start(bf16[16,3,128,128]{3,2,1,0:T(8,128)(2,1)} %by_heads.1), calls=%async_computation | async-start | bytes 3145728 | tf_op jit(solution)/shard_map/all_to_all | solution.py:371
  54.0 17.3 %collective-permute-start.9 = (bf16[512,128]{1,0:T(8,128)(2,1)S(1)}, bf16[512,128]{1,0:T(8,128)(2,1)S(1)}, u32[]{:S(2)}, u32[]{:S(2)}) collective-permute-start(bf16[512,128]{1,0:T(8,128)(2,1)S(1)} %get-tuple-element.83), channel_id=1, source_target_pairs={{0,64},{64,128},{128,192},{192,0},{1,65},{65,129},{129,193},{193,1... | collective-permute-start | bytes 393224 | tf_op jit(solution)/shard_map/ppermute | solution.py:375
  57.6 13.9 %collective-permute-start.10 = (bf16[512,128]{1,0:T(8,128)(2,1)S(1)}, bf16[512,128]{1,0:T(8,128)(2,1)S(1)}, u32[]{:S(2)}, u32[]{:S(2)}) collective-permute-start(bf16[512,128]{1,0:T(8,128)(2,1)S(1)} %get-tuple-element.84), channel_id=1, source_target_pairs={{0,192},{64,0},{128,64},{192,128},{1,193},{65,1},{129,65},{193,129... | collective-permute-start | bytes 393224 | tf_op jit(solution)/shard_map/ppermute | solution.py:375
  64.1 14.2 %collective-permute-start.8 = (bf16[512,128]{1,0:T(8,128)(2,1)S(1)}, bf16[512,128]{1,0:T(8,128)(2,1)S(1)}, u32[]{:S(2)}, u32[]{:S(2)}) collective-permute-start(bf16[512,128]{1,0:T(8,128)(2,1)S(1)} %get-tuple-element.86), channel_id=1, source_target_pairs={{0,128},{64,192},{128,0},{192,64},{1,129},{65,193},{129,1},{193,65... | collective-permute-start | bytes 393224 | tf_op jit(solution)/shard_map/ppermute | solution.py:375
  78.4 16.7 %collective-permute-start.13 = (bf16[128,512]{1,0:T(8,128)(2,1)S(1)}, bf16[128,512]{1,0:T(8,128)(2,1)S(1)}, u32[]{:S(2)}, u32[]{:S(2)}) collective-permute-start(bf16[128,512]{1,0:T(8,128)(2,1)S(1)} %get-tuple-element.80), channel_id=1, source_target_pairs={{0,48},{16,32},{32,16},{48,0},{1,49},{17,33},{33,17},{49,1},{2,50}... | collective-permute-start | bytes 393224 | tf_op jit(solution)/shard_map/ppermute | solution.py:379
  79.4 15.7 %collective-permute-start.12 = (bf16[128,512]{1,0:T(8,128)(2,1)S(1)}, bf16[128,512]{1,0:T(8,128)(2,1)S(1)}, u32[]{:S(2)}, u32[]{:S(2)}) collective-permute-start(bf16[128,512]{1,0:T(8,128)(2,1)S(1)} %get-tuple-element.81), channel_id=1, source_target_pairs={{0,32},{16,48},{32,0},{48,16},{1,33},{17,49},{33,1},{49,17},{2,34}... | collective-permute-start | bytes 393224 | tf_op jit(solution)/shard_map/ppermute | solution.py:379
  81.4 13.7 %collective-permute-start.11 = (bf16[128,512]{1,0:T(8,128)(2,1)S(1)}, bf16[128,512]{1,0:T(8,128)(2,1)S(1)}, u32[]{:S(2)}, u32[]{:S(2)}) collective-permute-start(bf16[128,512]{1,0:T(8,128)(2,1)S(1)} %get-tuple-element.82), channel_id=1, source_target_pairs={{0,16},{16,0},{32,48},{48,32},{1,17},{17,1},{33,49},{49,33},{2,18}... | collective-permute-start | bytes 393224 | tf_op jit(solution)/shard_map/ppermute | solution.py:379
  90.9 21.7 %collective-permute-start.15 = (bf16[2,288,128]{2,1,0:T(8,128)(2,1)S(1)}, bf16[2,288,128]{2,1,0:T(8,128)(2,1)S(1)}, u32[]{:S(2)}, u32[]{:S(2)}) collective-permute-start(bf16[2,288,128]{2,1,0:T(8,128)(2,1)S(1)} %get-tuple-element.77), channel_id=1, source_target_pairs={{0,64},{64,128},{128,192},{192,0},{1,65},{65,129},{129,193},{193,1... | collective-permute-start | bytes 442376 | tf_op jit(solution)/shard_map/ppermute | solution.py:375
  91.0 21.6 %collective-permute-start.14 = (bf16[2,288,128]{2,1,0:T(8,128)(2,1)S(1)}, bf16[2,288,128]{2,1,0:T(8,128)(2,1)S(1)}, u32[]{:S(2)}, u32[]{:S(2)}) collective-permute-start(bf16[2,288,128]{2,1,0:T(8,128)(2,1)S(1)} %get-tuple-element.78), channel_id=1, source_target_pairs={{0,192},{64,0},{128,64},{192,128},{1,193},{65,1},{129,65},{193,129... | collective-permute-start | bytes 442376 | tf_op jit(solution)/shard_map/ppermute | solution.py:375
  109.1 33.2 %collective-permute-start.22 = (bf16[288,512]{1,0:T(8,128)(2,1)S(1)}, bf16[288,512]{1,0:T(8,128)(2,1)S(1)}, u32[]{:S(2)}, u32[]{:S(2)}) collective-permute-start(bf16[288,512]{1,0:T(8,128)(2,1)S(1)} %get-tuple-element.69), channel_id=1, source_target_pairs={{0,48},{16,32},{32,16},{48,0},{1,49},{17,33},{33,17},{49,1},{2,50}... | collective-permute-start | bytes 884744 | tf_op jit(solution)/shard_map/ppermute | solution.py:379
  110.1 32.3 %collective-permute-start.21 = (bf16[288,512]{1,0:T(8,128)(2,1)S(1)}, bf16[288,512]{1,0:T(8,128)(2,1)S(1)}, u32[]{:S(2)}, u32[]{:S(2)}) collective-permute-start(bf16[288,512]{1,0:T(8,128)(2,1)S(1)} %get-tuple-element.70), channel_id=1, source_target_pairs={{0,32},{16,48},{32,0},{48,16},{1,33},{17,49},{33,1},{49,17},{2,34}... | collective-permute-start | bytes 884744 | tf_op jit(solution)/shard_map/ppermute | solution.py:379
  112.1 30.3 %collective-permute-start.20 = (bf16[288,512]{1,0:T(8,128)(2,1)S(1)}, bf16[288,512]{1,0:T(8,128)(2,1)S(1)}, u32[]{:S(2)}, u32[]{:S(2)}) collective-permute-start(bf16[288,512]{1,0:T(8,128)(2,1)S(1)} %get-tuple-element.71), channel_id=1, source_target_pairs={{0,16},{16,0},{32,48},{48,32},{1,17},{17,1},{33,49},{49,33},{2,18}... | collective-permute-start | bytes 884744 | tf_op jit(solution)/shard_map/ppermute | solution.py:379
  128.0 15.1 %collective-permute-start.19 = (bf16[4,288,128]{2,1,0:T(8,128)(2,1)S(1)}, bf16[4,288,128]{2,1,0:T(8,128)(2,1)S(1)}, u32[]{:S(2)}, u32[]{:S(2)}) collective-permute-start(bf16[4,288,128]{2,1,0:T(8,128)(2,1)S(1)} %get-tuple-element.75), channel_id=1, source_target_pairs={{0,64},{64,128},{128,192},{192,0},{1,65},{65,129},{129,193},{193,1... | collective-permute-start | bytes 884744 | tf_op jit(solution)/shard_map/ppermute | solution.py:375
  130.8 21.3 %collective-permute-start.16 = (bf16[4,288,128]{2,1,0:T(8,128)(2,1)S(1)}, bf16[4,288,128]{2,1,0:T(8,128)(2,1)S(1)}, u32[]{:S(2)}, u32[]{:S(2)}) collective-permute-start(bf16[4,288,128]{2,1,0:T(8,128)(2,1)S(1)} %get-tuple-element.76), channel_id=1, source_target_pairs={{0,192},{64,0},{128,64},{192,128},{1,193},{65,1},{129,65},{193,129... | collective-permute-start | bytes 884744 | tf_op jit(solution)/shard_map/ppermute | solution.py:375
  157.5 38.6 %all-to-all-start.1 = ((bf16[16,128,512]{2,1,0:T(8,128)(2,1)}), bf16[16,128,512]{2,1,0:T(8,128)(2,1)}, u32[]{:S(2)}, u32[]{:S(2)}) async-start(bf16[16,128,512]{2,1,0:T(8,128)(2,1)} %bitcast.77), calls=%async_computation.1 | async-start | bytes 4194304 | tf_op jit(solution)/shard_map/all_to_all | solution.py:371
  168.7 33.1 %collective-permute-start.23 = (bf16[4,160,128]{2,1,0:T(8,128)(2,1)}, bf16[4,160,128]{2,1,0:T(8,128)(2,1)}, u32[]{:S(2)}, u32[]{:S(2)}) collective-permute-start(bf16[4,160,128]{2,1,0:T(8,128)(2,1)} %get-tuple-element.54), channel_id=1, source_target_pairs={{0,192},{64,0},{128,64},{192,128},{1,193},{65,1},{129,65},{193,129... | collective-permute-start | bytes 491528 | tf_op jit(solution)/shard_map/ppermute | solution.py:375
  172.3 32.9 %collective-permute-start.24 = (bf16[4,160,128]{2,1,0:T(8,128)(2,1)}, bf16[4,160,128]{2,1,0:T(8,128)(2,1)S(1)}, u32[]{:S(2)}, u32[]{:S(2)}) collective-permute-start(bf16[4,160,128]{2,1,0:T(8,128)(2,1)} %get-tuple-element.55), channel_id=1, source_target_pairs={{0,128},{64,192},{128,0},{192,64},{1,129},{65,193},{129,1},{193,65... | collective-permute-start | bytes 491528 | tf_op jit(solution)/shard_map/ppermute | solution.py:375
  175.9 29.4 %collective-permute-start.25 = (bf16[4,160,128]{2,1,0:T(8,128)(2,1)}, bf16[4,160,128]{2,1,0:T(8,128)(2,1)S(1)}, u32[]{:S(2)}, u32[]{:S(2)}) collective-permute-start(bf16[4,160,128]{2,1,0:T(8,128)(2,1)} %get-tuple-element.56), channel_id=1, source_target_pairs={{0,64},{64,128},{128,192},{192,0},{1,65},{65,129},{129,193},{193,1... | collective-permute-start | bytes 491528 | tf_op jit(solution)/shard_map/ppermute | solution.py:375
  180.2 36.3 %collective-permute-start.29 = (bf16[2,128,2048]{2,1,0:T(8,128)(2,1)S(1)}, bf16[2,128,2048]{2,1,0:T(8,128)(2,1)}, u32[]{:S(2)}, u32[]{:S(2)}) collective-permute-start(bf16[2,128,2048]{2,1,0:T(8,128)(2,1)S(1)} %slice_bitcast_fusion.1), channel_id=1, source_target_pairs={{0,16},{16,0},{32,48},{48,32},{1,17},{17,1},{33,49},{49,33},{2,18}... | collective-permute-start | bytes 3145736 | tf_op jit(solution)/shard_map/ppermute | solution.py:379
  201.7 14.6 %collective-permute-start.31 = (bf16[128,512]{1,0:T(8,128)(2,1)S(1)}, bf16[128,512]{1,0:T(8,128)(2,1)S(1)}, u32[]{:S(2)}, u32[]{:S(2)}) collective-permute-start(bf16[128,512]{1,0:T(8,128)(2,1)S(1)} %reduce_sum.12), channel_id=1, source_target_pairs={{0,128},{64,192},{128,0},{192,64},{1,129},{65,193},{129,1},{193,65... | collective-permute-start | bytes 393224 | tf_op jit(solution)/shard_map/ppermute | solution.py:375
  205.3 11.1 %collective-permute-start.30 = (bf16[128,512]{1,0:T(8,128)(2,1)S(1)}, bf16[128,512]{1,0:T(8,128)(2,1)S(1)}, u32[]{:S(2)}, u32[]{:S(2)}) collective-permute-start(bf16[128,512]{1,0:T(8,128)(2,1)S(1)} %reduce_sum.12), channel_id=1, source_target_pairs={{0,64},{64,128},{128,192},{192,0},{1,65},{65,129},{129,193},{193,1... | collective-permute-start | bytes 393224 | tf_op jit(solution)/shard_map/ppermute | solution.py:375
  206.2 17.4 %collective-permute-start.26 = (bf16[4,160,128]{2,1,0:T(8,128)(2,1)S(1)}, bf16[4,160,128]{2,1,0:T(8,128)(2,1)S(1)}, u32[]{:S(2)}, u32[]{:S(2)}) collective-permute-start(bf16[4,160,128]{2,1,0:T(8,128)(2,1)S(1)} %pad_maximum_fusion.10), channel_id=1, source_target_pairs={{0,16},{16,0},{32,48},{48,32},{1,17},{17,1},{33,49},{49,33},{2,18}... | collective-permute-start | bytes 491528 | tf_op jit(solution)/shard_map/ppermute | solution.py:379
  218.2 32.4 %collective-permute-start.33 = (bf16[128,2048]{1,0:T(8,128)(2,1)S(1)}, bf16[128,2048]{1,0:T(8,128)(2,1)S(1)}, u32[]{:S(2)}, u32[]{:S(2)}) collective-permute-start(bf16[128,2048]{1,0:T(8,128)(2,1)S(1)} %fusion.3), channel_id=1, source_target_pairs={{0,32},{16,48},{32,0},{48,16},{1,33},{17,49},{33,1},{49,17},{2,34}... | collective-permute-start | bytes 1572872 | tf_op jit(solution)/shard_map/ppermute | solution.py:379
  218.4 18.2 %collective-permute-start.27 = (bf16[4,160,128]{2,1,0:T(8,128)(2,1)S(1)}, bf16[4,160,128]{2,1,0:T(8,128)(2,1)S(1)}, u32[]{:S(2)}, u32[]{:S(2)}) collective-permute-start(bf16[4,160,128]{2,1,0:T(8,128)(2,1)S(1)} %pad_maximum_fusion.11), channel_id=1, source_target_pairs={{0,32},{16,48},{32,0},{48,16},{1,33},{17,49},{33,1},{49,17},{2,34}... | collective-permute-start | bytes 491528 | tf_op jit(solution)/shard_map/ppermute | solution.py:379
  220.5 21.1 %collective-permute-start.28 = (bf16[4,160,128]{2,1,0:T(8,128)(2,1)S(1)}, bf16[4,160,128]{2,1,0:T(8,128)(2,1)S(1)}, u32[]{:S(2)}, u32[]{:S(2)}) collective-permute-start(bf16[4,160,128]{2,1,0:T(8,128)(2,1)S(1)} %pad_maximum_fusion.12), channel_id=1, source_target_pairs={{0,48},{16,32},{32,16},{48,0},{1,49},{17,33},{33,17},{49,1},{2,50}... | collective-permute-start | bytes 491528 | tf_op jit(solution)/shard_map/ppermute | solution.py:379
  222.0 25.1 %collective-permute-start.36 = (bf16[128,512]{1,0:T(8,128)(2,1)S(1)}, bf16[128,512]{1,0:T(8,128)(2,1)S(1)}, u32[]{:S(2)}, u32[]{:S(2)}) collective-permute-start(bf16[128,512]{1,0:T(8,128)(2,1)S(1)} %add_convert_fusion.refs_0_), channel_id=1, source_target_pairs={{0,48},{16,32},{32,16},{48,0},{1,49},{17,33},{33,17},{49,1},{2,50}... | collective-permute-start | bytes 393224 | tf_op jit(solution)/shard_map/ppermute | solution.py:379
  223.6 23.5 %collective-permute-start.35 = (bf16[128,512]{1,0:T(8,128)(2,1)S(1)}, bf16[128,512]{1,0:T(8,128)(2,1)S(1)}, u32[]{:S(2)}, u32[]{:S(2)}) collective-permute-start(bf16[128,512]{1,0:T(8,128)(2,1)S(1)} %add_convert_fusion.refs_0_), channel_id=1, source_target_pairs={{0,32},{16,48},{32,0},{48,16},{1,33},{17,49},{33,1},{49,17},{2,34}... | collective-permute-start | bytes 393224 | tf_op jit(solution)/shard_map/ppermute | solution.py:379
  236.6 10.5 %collective-permute-start.34 = (bf16[128,512]{1,0:T(8,128)(2,1)S(1)}, bf16[128,512]{1,0:T(8,128)(2,1)S(1)}, u32[]{:S(2)}, u32[]{:S(2)}) collective-permute-start(bf16[128,512]{1,0:T(8,128)(2,1)S(1)} %add_convert_fusion.refs_0_), channel_id=1, source_target_pairs={{0,16},{16,0},{32,48},{48,32},{1,17},{17,1},{33,49},{49,33},{2,18}... | collective-permute-start | bytes 393224 | tf_op jit(solution)/shard_map/ppermute | solution.py:379
  (34 other events, 559.2 us)
